TPU v7x, 128 devices: a whole 4x4x4 slice. The times are simulated.
128 devices in a mesh: group: 4 (over x), seq: 32 (over y, z, core).
Axes of the slice: x: 4, y: 4, z: 4, core: 2. Of those that a mesh axis runs over, the one named last changes fastest.
Arguments:
- layer_input: bfloat16 [4, 24576, 5120], P('group', 'seq'), may hold values from -6 to 6
- x_values: bfloat16 [4, 24576, 2560], P('group', 'seq'), may hold values from -6 to 6
- out_grad: bfloat16 [4, 24576, 2560], P('group', 'seq'), may hold values from -0.29882812 to 0.29882812
- b_values: bfloat16 [4, 24576, 128], P('group', 'seq'), may hold values from -0.3 to 0.3
- c_values: bfloat16 [4, 24576, 128], P('group', 'seq'), may hold values from -0.29882812 to 0.29882812
- step_sizes: float32 [4, 40, 24576], P('group', None, 'seq'), may hold values from 0.5 to 36866
- decay_rates: float32 [40], replicated, may hold values from 4.06901042e-06 to 0.06
- prompt_state: float32 [4, 2560, 128], P('group', 'seq'), may hold values from -6 to 6
- lengths: int32 [4, 4], P('group'), may hold values from 1 to 48, 96 in all within a row
Outputs:
- x_grad: bfloat16 [4, 24576, 2560], P('group', 'seq')
- prompt_grad: float32 [4, 2560, 128], P('group', 'seq')
- weight_grad: float32 [5120, 256], P(('group', 'seq'))
Inputs may be any that keep to these rules, and one draw needn't show every extreme that they name: The 4 lengths of a prompt sum to 96, and the longest is exactly 48.
All inputs are finite; a program needn't handle non-finite values.
Results may differ from a plain program's by a relative error of at most 0.0062.
Values sent between devices are 32-bit elements; how exact they have to be, the bound alone decides.
A program may use at most 320 MiB of HBM per device.

v0:
```python
from functools import partial

import jax
import jax.numpy as jnp
from jax import lax
from jax.sharding import PartitionSpec as P

BLOCK = 256


def carried_in(value, axis, combine, identity, reverse):
    size, position = (lax.axis_size(axis), lax.axis_index(axis))
    everything = jax.tree.map(lambda part: lax.all_gather(part, axis), value)
    start = jax.tree.map(
        lambda part, zero: jnp.broadcast_to(jnp.asarray(zero, part.dtype), part.shape),
        value,
        identity,
    )

    def step(k, before):
        at = size - 1 - k if reverse else k
        reached = at > position if reverse else at < position
        new = combine(before, jax.tree.map(lambda part: part[at], everything))
        return jax.tree.map(lambda a, b: jnp.where(reached, a, b), new, before)

    return lax.fori_loop(0, size, step, start)


def block_logs(step_block, decay_rates):
    return jnp.cumsum(-step_block * decay_rates[:, None], axis=1)


def summarize(x_block, grad_block, b_block, c_block, step_block, decay_rates):
    log_decay = block_logs(step_block, decay_rates)
    block_end = log_decay[:, -1:]
    rescaled_input = (x_block * (jnp.exp(block_end - log_decay) * step_block).T[:, :, None]).astype(
        jnp.bfloat16
    )
    rescaled_gradient = (grad_block * jnp.exp(log_decay).T[:, :, None]).astype(jnp.bfloat16)
    local_state = jnp.einsum(
        "lhp,ln->hpn", rescaled_input, b_block, preferred_element_type=jnp.float32
    )
    local_grad = jnp.einsum(
        "lhp,ln->hpn", rescaled_gradient, c_block, preferred_element_type=jnp.float32
    )
    return (jnp.exp(block_end[:, 0]), rescaled_input, rescaled_gradient, local_state, local_grad)


def process(
    x_block,
    grad_block,
    b_block,
    c_block,
    step_block,
    rescaled_input,
    rescaled_gradient,
    entering,
    leaving,
    decay_rates,
):
    log_decay = block_logs(step_block, decay_rates)
    block_end = log_decay[:, -1:]
    width = step_block.shape[1]
    places = jnp.arange(width)
    causal = places[:, None] >= places[None, :]
    gap_matrix = log_decay[:, :, None] - log_decay[:, None, :]
    masked = jnp.exp(jnp.where(causal[None], gap_matrix, -jnp.inf))
    products = jnp.einsum("thp,shp->hts", grad_block, x_block, preferred_element_type=jnp.float32)
    inner = jnp.einsum("sn,tn->st", c_block, b_block, preferred_element_type=jnp.float32)
    dx_weights = (masked * inner[None]).astype(jnp.bfloat16)
    leaving_low = leaving.astype(jnp.bfloat16)
    entering_low = entering.astype(jnp.bfloat16)
    dx_inner = jnp.einsum(
        "hst,shp->thp", dx_weights, grad_block, preferred_element_type=jnp.float32
    )
    dx_outer = jnp.einsum("tn,hpn->thp", b_block, leaving_low, preferred_element_type=jnp.float32)
    x_grad = step_block.T[:, :, None] * (
        dx_inner + jnp.exp(block_end - log_decay).T[:, :, None] * dx_outer
    )
    pair_weights = jnp.sum(masked * products * step_block[:, None, :], axis=0).astype(jnp.bfloat16)
    b_gradient = jnp.einsum(
        "st,sn->tn", pair_weights, c_block, preferred_element_type=jnp.float32
    ) + jnp.einsum("thp,hpn->tn", rescaled_input, leaving_low, preferred_element_type=jnp.float32)
    readout_gradient = jnp.einsum(
        "ts,sn->tn", pair_weights, b_block, preferred_element_type=jnp.float32
    ) + jnp.einsum(
        "thp,hpn->tn", rescaled_gradient, entering_low, preferred_element_type=jnp.float32
    )
    return (
        x_grad.astype(jnp.bfloat16),
        jnp.concatenate([b_gradient, readout_gradient], axis=1).astype(jnp.bfloat16),
    )


def group_flags(sample_lengths, block_ids):
    sample_ends = jnp.cumsum(sample_lengths)
    sample_starts = sample_ends - sample_lengths
    is_start = jnp.any(sample_starts[:, None] == block_ids[None, :], axis=0)
    is_last = jnp.any((sample_ends - 1)[:, None] == block_ids[None, :], axis=0)
    return (is_start, is_last)


def combine(earlier, later):
    return (earlier[0] * later[0], later[0][:, None, None] * earlier[1] + later[1])


def compose_step(carry, items):
    return (combine(carry, items), None)


def forward_step(prompt, carry, items):
    start, decay, local = items
    entering = jnp.where(start, prompt, carry)
    return (decay[:, None, None] * entering + local, entering)


def backward_step(carry, items):
    last, decay, local = items
    leaving = jnp.where(last, jnp.zeros_like(carry), carry)
    passed = decay[:, None, None] * leaving + local
    return (passed, (leaving, passed))


def body(
    layer_input,
    x_values,
    out_grad,
    b_values,
    c_values,
    step_sizes,
    decay_rates,
    prompt_state,
    lengths,
):
    tok_count = x_values.shape[1]
    n_blocks = tok_count // BLOCK
    num_heads = decay_rates.shape[0]
    head_size = x_values.shape[2] // num_heads
    state_size = b_values.shape[2]
    x_blocks = x_values[0].reshape(n_blocks, BLOCK, num_heads, head_size)
    grad_blocks = out_grad[0].reshape(n_blocks, BLOCK, num_heads, head_size)
    b_blocks = b_values[0].reshape(n_blocks, BLOCK, state_size)
    c_blocks = c_values[0].reshape(n_blocks, BLOCK, state_size)
    step_blocks = step_sizes[0].reshape(num_heads, n_blocks, BLOCK).transpose(1, 0, 2)
    prompt = lax.all_gather(prompt_state[0], "seq", axis=0, tiled=True).reshape(
        num_heads, head_size, state_size
    )
    block_ids = lax.axis_index("seq") * n_blocks + jnp.arange(n_blocks)
    is_start, is_last = group_flags(lengths[0], block_ids)
    decays, rescaled_input, rescaled_gradient, local_state, local_grad = lax.map(
        lambda items: summarize(*items, decay_rates),
        (x_blocks, grad_blocks, b_blocks, c_blocks, step_blocks),
    )
    fwd_decay = jnp.where(is_start[:, None], 0.0, decays)
    fwd_value = (
        local_state + jnp.where(is_start[:, None], decays, 0.0)[:, :, None, None] * prompt[None]
    )
    back_decay = jnp.where(is_last[:, None], 0.0, decays)
    unit_decay = jnp.ones((num_heads,), jnp.float32)
    zeros = jnp.zeros((num_heads, head_size, state_size), jnp.float32)
    fwd_total, _ = lax.scan(compose_step, (unit_decay, zeros), (fwd_decay, fwd_value))
    back_total, _ = lax.scan(
        compose_step, (unit_decay, zeros), (back_decay, local_grad), reverse=True
    )
    entering_device = carried_in(
        (fwd_total[0], fwd_total[1]), "seq", combine, (unit_decay, zeros), False
    )[1]
    leaving_device = carried_in(
        (back_total[0], back_total[1]), "seq", combine, (unit_decay, zeros), True
    )[1]
    _, entering = lax.scan(
        partial(forward_step, prompt), entering_device, (is_start, decays, local_state)
    )
    _, (leaving, passed) = lax.scan(
        backward_step, leaving_device, (is_last, decays, local_grad), reverse=True
    )
    prompt_term = jnp.sum(
        jnp.where(is_start[:, None, None, None], passed, jnp.zeros_like(passed)), axis=0
    )
    prompt_term = prompt_term.reshape(num_heads * head_size, state_size)
    x_grad, bc_grad = lax.map(
        lambda items: process(*items, decay_rates),
        (
            x_blocks,
            grad_blocks,
            b_blocks,
            c_blocks,
            step_blocks,
            rescaled_input,
            rescaled_gradient,
            entering,
            leaving,
        ),
    )
    bc_rows = bc_grad.reshape(tok_count, 2 * state_size)
    input_rows = layer_input[0]
    weight_grad = lax.psum_scatter(
        jnp.einsum("td,tk->dk", input_rows, bc_rows, preferred_element_type=jnp.float32),
        ("group", "seq"),
        scatter_dimension=0,
        tiled=True,
    )
    prompt_grad = lax.psum_scatter(prompt_term, "seq", scatter_dimension=0, tiled=True)
    return (x_grad.reshape(1, tok_count, num_heads * head_size), prompt_grad[None], weight_grad)


def solution(mesh):
    in_specs = (
        P("group", "seq", None),
        P("group", "seq", None),
        P("group", "seq", None),
        P("group", "seq", None),
        P("group", "seq", None),
        P("group", None, "seq"),
        P(),
        P("group", "seq", None),
        P("group", None),
    )
    out_specs = (P("group", "seq", None), P("group", "seq", None), P(("group", "seq"), None))
    return jax.shard_map(body, mesh=mesh, in_specs=in_specs, out_specs=out_specs, check_vma=False)
```

profile of v0, /device:TPU:0, one launch (start us, length us, event | category | flops | bytes accessed | tf_op | source)
XLA Modules:
  0.0 1164.2 jit_solution(12162671959375716028)
XLA Ops:
  8.0 10.7 reshape.217
  18.7 11.3 copy.77
  30.0 10.7 reshape.216
  40.7 11.3 copy.80
  52.1 2.4 broadcast.70.clone
  54.5 2.5 broadcast.70.clone.1
  57.1 2.4 broadcast.73.clone
  59.5 2.4 broadcast.73.clone.1
  61.9 34.0 %while.128 = (s32[]{:T(128)}, f32[3,40]{1,0:T(4,128)S(1)}, bf16[3,256,40,64]{1,3,2,0:T(8,128)(2,1)}, bf16[3,256,40,64]{1,3,2,0:T(8,128)(2,1)}, f32[3,40,64,128]{...) while((s32[]{:T(128)}, f32[3,40]{1,0:T(4,128)S(1)}, ...), condition=%wide.region_3.4_spmd.clone, body=%wide.region_0.3_spmd.sunk.clone | while | flops 344770688 | bytes 11361673 | solution.py:150
  63.2 4.2 fusion.162
  67.4 2.9 fusion.163
  70.3 2.9 fusion.164
  74.5 4.2 fusion.162
  78.7 2.9 fusion.163
  81.6 2.9 fusion.164
  85.8 4.2 fusion.162
  90.0 2.9 fusion.163
  92.9 2.9 fusion.164
  96.7 4.7 while.132
  102.7 4.8 multiply_add_fusion
  107.4 4.7 while.134
  118.1 132.4 %all-reduce.2 = (f32[1280]{0:T(1024)}, f32[1280]{0:T(1024)}) all-reduce(f32[1280]{0:T(1024)S(1)} %dynamic-update-slice, f32[1280]{0:T(1024)S(1)} %dynamic-update-slice.1), channel_id=2, replica_groups=mesh['group'=4,'seq'=32] {'seq'}, use_global_device_ids=true, to_apply=%add | all-reduce | flops 2560 | bytes 20480
  252.7 75.8 %while.133 = (s32[]{:T(128)}, f32[40,64,128]{2,1,0:T(8,128)S(1)}, s32[]{:T(128)}, f32[32,40]{1,0:T(8,128)}, f32[32,40,64,128]{3,2,1,0:T(8,128)}) while((s32[]{:T(128)}, f32[40,64,128]{2,1,0:T(8,128)S(1)}, s32[]{:T(128)}, f32[32,40]{1,0:T(8,128)}, f32[32,40,64,128]{3,2,1,0:T(8,128)}) %tuple.306), condition=%wide.region_16.17_spmd.clone.clone, body=%wide.region_15.16_spmd.clone.sunk.clone | while | flops 1310728 | bytes 3932775 | solution.py:26
  328.6 2.3 broadcast.73
  330.9 21.0 %while.129 = (s32[]{:T(128)}, f32[40,64,128]{2,1,0:T(8,128)S(1)}, bf16[3,40,64,128]{3,2,1,0:T(8,128)(2,1)}, f32[3,40,64,128]{3,2,1,0:T(8,128)}, f32[3,40]{1,0:T(...) while((s32[]{:T(128)}, f32[40,64,128]{2,1,0:T(8,128)S(1)}, ...), condition=%wide.region_18.19_spmd.clone, body=%wide.region_17.18_spmd.sunk.clone | while | flops 1310723 | bytes 7210571 | solution.py:174
  334.5 3.4 bitcast_dynamic-update-slice_fusion.9
  341.5 3.4 bitcast_dynamic-update-slice_fusion.9
  348.6 3.4 bitcast_dynamic-update-slice_fusion.9
  351.9 3.9 select_reduce_fusion
  356.1 23.2 %all-gather.13.cloned.1.call-done = f32[1280,64,128]{2,1,0:T(8,128)} async-done(((f32[40,64,128]{2,1,0:T(8,128)}), f32[1280,64,128]{2,1,0:T(8,128)}) %all-gather.13.cloned.1.call-update) | async-done | bytes 41943056 | tf_op jit(solution)/shard_map/all_gather | solution.py:13
  379.3 53.4 %while.135 = (s32[]{:T(128)}, f32[40,64,128]{2,1,0:T(8,128)S(1)}, s32[]{:T(128)}, f32[32,40]{1,0:T(8,128)S(1)}, f32[32,40,64,128]{3,2,1,0:T(8,128)}) while((s32[]{:T(128)}, f32[40,64,128]{2,1,0:T(8,128)S(1)}, s32[]{:T(128)}, f32[32,40]{1,0:T(8,128)S(1)}, f32[32,40,64,128]{3,2,1,0:T(8,128)}) %tuple.305), condition=%wide.region_9.10_spmd.clone.clone, body=%wide.region_8.9_spmd.clone.sunk.clone | while | flops 1310724 | bytes 3932729 | solution.py:26
  432.7 17.8 %while.130 = (s32[]{:T(128)}, f32[40,64,128]{2,1,0:T(8,128)S(1)}, bf16[3,40,64,128]{3,2,1,0:T(8,128)(2,1)}, f32[3,40]{1,0:T(4,128)}, pred[3]{0:T(512)(128)(4,1)}...) while((s32[]{:T(128)}, f32[40,64,128]{2,1,0:T(8,128)S(1)}, ...), condition=%wide.region_11.12_spmd.clone, body=%wide.region_10.11_spmd.sunk.clone | while | flops 1310722 | bytes 8521276 | solution.py:171
  436.4 2.2 bitcast_add_fusion.15
  442.4 2.2 bitcast_add_fusion.15
  448.3 2.2 bitcast_add_fusion.15
  450.5 2.4 broadcast.70
  452.9 47.6 %while.131 = (s32[]{:T(128)}, bf16[3,256,40,64]{1,3,2,0:T(8,128)(2,1)}, bf16[3,256,256]{2,1,0:T(8,128)(2,1)S(1)}, f32[3,40,256]{2,1,0:T(8,128)S(1)}, bf16[3,256,...) while((s32[]{:T(128)}, ...), condition=%wide.region_23.24_spmd.clone, body=%wide.region_19.23_spmd.sunk.clone | while | flops 1252696192 | bytes 34555344 | solution.py:181
  456.0 3.8 fusion.184
  459.8 4.8 multiply_reduce_fusion.3
  471.8 3.8 fusion.184
  475.6 4.8 multiply_reduce_fusion.3
  487.7 3.8 fusion.184
  491.5 4.8 multiply_reduce_fusion.3
  500.5 7.8 fusion.81
  508.3 5.9 copy.87
  514.3 11.4 copy.86
  525.7 11.1 reshape.213
  536.8 620.9 %reduce-scatter.7.cloned.1.call-done = f32[40,256]{1,0:T(8,128)} async-done(((f32[5120,256]{1,0:T(8,128)}), f32[40,256]{1,0:T(8,128)}) %reduce-scatter.7.cloned.1.call-update) | async-done | bytes 40976
  (324 shorter events, 194.8 us)
Async XLA Ops:
  7.2 95.5 %all-gather.11.cloned.1.call-start = ((), (), s32[]{:S(2)}) async-start(), calls=%async_computation.4 | async-start | bytes 1351680 | tf_op jit(solution)/shard_map/all_gather | solution.py:145
  7.9 244.8 %all-gather.9.cloned.1.call-start = ((), (), s32[]{:S(2)}) async-start(), calls=%async_computation.3 | async-start | bytes 43253760 | tf_op jit(solution)/shard_map/all_gather | solution.py:13
  40.7 11.3 copy-start.8
  59.5 2.4 copy-start.6
  59.5 2.4 copy-start.7
  59.5 2.4 copy-start.9
  61.8 34.0 %copy-start.14 = (s32[1,4]{1,0:T(1,128)S(1)}, s32[1,4]{1,0:T(1,128)}, u32[]{:S(2)}) copy-start(s32[1,4]{1,0:T(1,128)} %param.33) | copy-start | bytes 52
  95.8 0.9 copy-start.13
  96.1 0.6 copy-start.10
  96.1 0.6 copy-start.12
  101.4 1.1 copy-start.4
  102.6 276.7 %all-gather.13.cloned.1.call-start = ((), (), s32[]{:S(2)}) async-start(), calls=%async_computation.5 | async-start | bytes 43253760 | tf_op jit(solution)/shard_map/all_gather | solution.py:13
  112.1 1.1 copy-start.5
  113.2 423.5 %reduce-scatter.5.cloned.1.call-start = ((), (), s32[]{:S(2)}) async-start(), calls=%async_computation.2 | async-start | bytes 1351680 | tf_op jit(solution)/shard_map/reduce_scatter | solution.py:203
  113.3 3.0 copy-start.15
  113.8 1.3 copy-start.2
  330.9 21.0 %copy-start.11 = (pred[3]{0:T(512)(128)(4,1)S(1)}, pred[3]{0:T(512)(128)(4,1)}, u32[]{:S(2)}) copy-start(pred[3]{0:T(512)(128)(4,1)} %copy-done.10) | copy-start | bytes 13
  355.9 801.8 %reduce-scatter.7.cloned.1.call-start = ((), (), s32[]{:S(2)}) async-start(), calls=%async_computation.6 | async-start | bytes 5283840
  379.3 53.4 %copy-start = (f32[1,2560,128]{2,1,0:T(8,128)S(1)}, f32[1,2560,128]{2,1,0:T(8,128)}, u32[]{:S(2)}) copy-start(f32[1,2560,128]{2,1,0:T(8,128)} %all-gather.11.cloned.1.call-done) | copy-start | bytes 3932164
  450.5 2.4 copy-start.3
  453.8 2.1 copy-start.1
  469.7 2.1 copy-start.1
  485.6 2.1 copy-start.1
Sparse Core Ops, SparseCore 0:
  10.2 45.6 all-gather.10
  102.7 139.4 all-gather.8
  244.4 134.7 all-gather.12
  383.2 77.3 reduce-scatter.4
  514.4 643.1 reduce-scatter.6
where the time goes:
time: 1170 us; the launch traced here: 1160 us
  waiting for transfers between devices  645 us (55%)
  other arithmetic  169 us (14%)
  local copies, waits for them, and re-layouts  136 us (12%)
  blocking collectives  132 us (11%)
  matrix products  65.1 us (6%)
  between operations  14.7 us (1%)
    unnamed x6, waiting for transfers between devices  622 us
    unnamed x1, blocking collectives  132 us
    select_n x64, other arithmetic, step(): return jax.tree.map(lambda a, b: jnp.where(reached, a, b), new, before)  105 us
    unnamed x39, local copies, waits for them, and re-layouts  34.8 us
    dynamic_update_slice x12, other arithmetic, body(): lax.map(lambda items: summarize(*items, decay_rates), (x_blocks, grad_blo...  32.9 us
  transfers between devices with their start and end apart: 5, of which 2 were waited for; matrix products, arithmetic and copies ran while one was open for 31% of the time, Pallas kernels for 0%

commit v1 on v0

v1 whole, which is shorter than its diff:
```python
from functools import partial

import jax
import jax.numpy as jnp
from jax import lax
from jax.experimental import pallas as pl
from jax.experimental.pallas import tpu as pltpu
from jax.sharding import PartitionSpec as P

BLOCK = 256
NBLK = 3
TOK = BLOCK * NBLK
HEADS = 40
PAIRS = HEADS // 2
STATE = 128
WIDTH = 2560
DMODEL = 5120
CHUNK = 80
MESSAGE = 3 * CHUNK + 8
F32 = jnp.float32
BF16 = jnp.bfloat16
MESH = pl.DeviceIdType.MESH
TN = (((0,), (0,)), ((), ()))
NT = (((1,), (1,)), ((), ()))
VMEM_LIMIT = 56 * 1024 * 1024


def dot(a, b, dims=(((1,), (0,)), ((), ()))):
    return lax.dot_general(a, b, dims, preferred_element_type=F32)


def iota(shape, dim):
    return lax.broadcasted_iota(jnp.int32, shape, dim)


def flags(lens_ref):
    first = lax.axis_index("seq") * NBLK
    e1 = lens_ref[0, 0]
    e2 = e1 + lens_ref[0, 1]
    e3 = e2 + lens_ref[0, 2]
    e4 = e3 + lens_ref[0, 3]
    not_start, not_last = [], []
    for k in range(NBLK):
        at = first + k
        start = (at == 0) | (at == e1) | (at == e2) | (at == e3)
        last = (at == e1 - 1) | (at == e2 - 1) | (at == e3 - 1) | (at == e4 - 1)
        not_start.append(jnp.where(start, 0.0, 1.0).astype(F32))
        not_last.append(jnp.where(last, 0.0, 1.0).astype(F32))
    return not_start, not_last


def parts_of(value, count):
    out = []
    for _ in range(count):
        high = value.astype(BF16).astype(F32)
        out.append(high)
        value = value - high
    return out


def columns(value, count):
    pieces = parts_of(value, count)
    pieces.append(jnp.zeros((128 - HEADS * count, value.shape[1]), F32))
    return jnp.concatenate(pieces, axis=0).T.astype(BF16)


def selector(first_head, count, lanes_per_head, width):
    row, lane = iota((128, width), 0), iota((128, width), 1)
    head = first_head + lane // lanes_per_head
    hit = row == head
    for n in range(1, count):
        hit = hit | (row == head + HEADS * n)
    return jnp.where(hit, 1.0, 0.0).astype(BF16)


def pair_decays(la_ref, pair):
    out = []
    rows = [la_ref[pl.ds(2 * pair + j, 1), :] for j in range(2)]
    for k in range(NBLK):
        at = BLOCK * (k + 1) - 1
        out.append(
            jnp.concatenate(
                [jnp.broadcast_to(jnp.exp(r[:, at : at + 1]), (64, 128)) for r in rows], axis=0
            )
        )
    return out


def summary_kernel(
    lens_ref, step_ref, rate_ref, x_ref, g_ref, b_ref, c_ref,
    f_ref, r_ref, u_ref, loc_ref, coef_ref, la_ref, w3_ref, s2_ref, x2_ref, g2_ref, all_ref,
):
    pair = pl.program_id(0)
    ns, nl = flags(lens_ref)

    @pl.when(pair == 0)
    def _():
        step = step_ref[...]
        la = -step * rate_ref[...]
        place = iota((HEADS, TOK), 1) % BLOCK
        shift = 1
        while shift < BLOCK:
            la = la + jnp.where(place >= shift, pltpu.roll(la, shift, 1), 0.0)
            shift *= 2
        la_ref[...] = la
        ends = [la[:, BLOCK * (k + 1) - 1 : BLOCK * (k + 1)] for k in range(NBLK)]
        end = jnp.concatenate([jnp.broadcast_to(e, (HEADS, BLOCK)) for e in ends], axis=1)
        w3_ref[...] = columns(la, 3)
        s2_ref[...] = columns(step, 2)
        x2_ref[...] = columns(jnp.exp(end - la) * step, 2)
        g2_ref[...] = columns(jnp.exp(la), 2)
        dec = [jnp.broadcast_to(jnp.exp(e), (HEADS, 128)) for e in ends]
        af = jnp.ones((HEADS, 128), F32)
        pc = jnp.zeros((HEADS, 128), F32)
        for k in range(NBLK):
            af = af * dec[k] * ns[k]
            pc = dec[k] * (pc * ns[k] + (1.0 - ns[k]))
        ab = jnp.ones((HEADS, 128), F32)
        uc = jnp.zeros((HEADS, 128), F32)
        for k in reversed(range(NBLK)):
            ab = ab * dec[k] * nl[k]
            uc = uc + ab * (1.0 - ns[k])
        for n, value in enumerate((af, pc, ab, uc)):
            all_ref[n] = value
        for o in range(32):
            h = CHUNK * o // 64
            for n in range(4):
                coef_ref[o, 2 * n : 2 * n + 2, :] = all_ref[n, h : h + 2, :]

    sel = selector(2 * pair, 2, 64, 128)
    sx = (x_ref[...].astype(F32) * dot(x2_ref[...], sel)).astype(BF16)
    sg = (g_ref[...].astype(F32) * dot(g2_ref[...], sel)).astype(BF16)
    dec = pair_decays(la_ref, pair)
    ls, lg = [], []
    for k in range(NBLK):
        rows = slice(BLOCK * k, BLOCK * (k + 1))
        ls.append(dot(sx[rows], b_ref[rows, :], TN))
        lg.append(dot(sg[rows], c_ref[rows, :], TN))
    f = ls[0]
    for k in range(1, NBLK):
        f = (dec[k] * ns[k]) * f + ls[k]
    f_ref[...] = f
    r = lg[2]
    u = r * (1.0 - ns[2])
    for k in (1, 0):
        r = dec[k] * (r * nl[k]) + lg[k]
        u = u + r * (1.0 - ns[k])
    r_ref[...] = r
    u_ref[...] = u
    loc_ref[0] = ls[0]
    loc_ref[1] = ls[1]
    loc_ref[2] = lg[1]
    loc_ref[3] = lg[2]


def summarize(lens, step, rates, x, g, b, c):
    whole = lambda *shape: pl.BlockSpec(shape, lambda i: (0,) * len(shape))
    lanes = pl.BlockSpec((TOK, 128), lambda i: (0, i))
    rows = pl.BlockSpec((128, 128), lambda i: (i, 0))
    state = jax.ShapeDtypeStruct((WIDTH, STATE), F32)
    cols = jax.ShapeDtypeStruct((TOK, 128), BF16)
    return pl.pallas_call(
        summary_kernel,
        grid=(PAIRS,),
        in_specs=[
            pl.BlockSpec(memory_space=pltpu.SMEM),
            whole(HEADS, TOK), whole(HEADS, 1), lanes, lanes, whole(TOK, 128), whole(TOK, 128),
        ],
        out_specs=[
            rows, rows, rows, pl.BlockSpec((4, 128, 128), lambda i: (0, i, 0)),
            whole(32, 8, 128), whole(HEADS, TOK),
            whole(TOK, 128), whole(TOK, 128), whole(TOK, 128), whole(TOK, 128),
        ],
        out_shape=[
            state, state, state, jax.ShapeDtypeStruct((4, WIDTH, STATE), F32),
            jax.ShapeDtypeStruct((32, 8, 128), F32), jax.ShapeDtypeStruct((HEADS, TOK), F32),
            cols, cols, cols, cols,
        ],
        scratch_shapes=[pltpu.VMEM((4, HEADS, 128), F32)],
        compiler_params=pltpu.CompilerParams(vmem_limit_bytes=VMEM_LIMIT),
    )(lens, step, rates, x, g, b, c)


def inside_unit(u, x_v, g_v, b_ref, c_ref, la_ref, w3_ref, s2_ref, inner_v, pt_v, dx_v):
    k, pair = u // PAIRS, u % PAIRS
    r = pl.ds(pl.multiple_of(k * BLOCK, BLOCK), BLOCK)
    l = pl.ds(pl.multiple_of(pair * 128, 128), 128)

    @pl.when(pair == 0)
    def _():
        keep = iota((BLOCK, BLOCK), 1) >= iota((BLOCK, BLOCK), 0)
        inner_v[...] = jnp.where(keep, dot(b_ref[r, :], c_ref[r, :], NT), 0.0)
        pt_v[k] = jnp.zeros((BLOCK, BLOCK), F32)

    g = g_v[r, l]
    col = dot(w3_ref[r, :], selector(2 * pair, 3, 128, 256))
    xs = (x_v[r, l].astype(F32) * dot(s2_ref[r, :], selector(2 * pair, 2, 64, 128))).astype(BF16)
    lane = iota((1, 128), 1)
    a00 = a01 = a11 = d0 = d1 = None
    plus = lambda a, b: b if a is None else a + b
    for j in range(2):
        gj = g * jnp.where((lane >= 64) == bool(j), 1.0, 0.0).astype(BF16)
        p0 = dot(xs[:128], gj, NT)
        p1 = dot(xs[128:], gj[128:], NT)
        row = la_ref[pl.ds(2 * pair + j, 1), r]
        cj = col[:, 128 * j : 128 * (j + 1)]
        q00 = jnp.exp(jnp.minimum(row[:, :128] - cj[:128], 0.0))
        q01 = jnp.exp(jnp.minimum(row[:, 128:] - cj[:128], 0.0))
        q11 = jnp.exp(jnp.minimum(row[:, 128:] - cj[128:], 0.0))
        a00 = plus(a00, q00 * p0[:, :128])
        a01 = plus(a01, q01 * p0[:, 128:])
        a11 = plus(a11, q11 * p1)
        w00 = (q00 * inner_v[:128, :128]).astype(BF16)
        w01 = (q01 * inner_v[:128, 128:]).astype(BF16)
        w11 = (q11 * inner_v[128:, 128:]).astype(BF16)
        d0 = plus(d0, dot(jnp.concatenate([w00, w01], axis=1), gj))
        d1 = plus(d1, dot(w11, gj[128:]))
    pt_v[k, :128, :128] += a00
    pt_v[k, :128, 128:] += a01
    pt_v[k, 128:, 128:] += a11
    dx_v[r, l] = jnp.concatenate([d0, d1], axis=0).astype(BF16)


def spread(tile, n, split):
    return jnp.where(iota((CHUNK, 128), 0) < split, tile[2 * n : 2 * n + 1], tile[2 * n + 1 : 2 * n + 2])


def split_of(owner):
    return 64 - (CHUNK * owner) % 64


def carry_kernel(
    f_ref, r_ref, u_ref, coef_ref, p_ref, x_hbm, g_hbm, b_ref, c_ref, la_ref, w3_ref, s2_ref,
    e_ref, l_ref, pr_ref, pg_ref, pt_ref, dx_hbm,
    x_v, g_v, dx_v, inner_v, pt_v,
    sf, sr, su, sc, prompts, comb, got, back, ret, sib_e, sib_l, sib_p,
    load_sem, sib_send, sib_recv, p_send, p_recv, a_send, a_recv, b_send, b_recv,
):
    group, seq = lax.axis_index("group"), lax.axis_index("seq")
    core = seq % 2
    chip = seq // 2
    y, z = chip // 4, chip % 4
    sibling = (group, chip * 2 + (1 - core))

    def peer(d):
        return (group, (((y + d // 4) % 4) * 4 + (z + d % 4) % 4) * 2 + core)

    def send(src, dst, s, r, to):
        return pltpu.make_async_remote_copy(
            src_ref=src, dst_ref=dst, send_sem=s, recv_sem=r, device_id=to, device_id_type=MESH
        )

    loads = [
        pltpu.make_async_copy(x_hbm, x_v, load_sem.at[0]),
        pltpu.make_async_copy(g_hbm, g_v, load_sem.at[1]),
    ]
    for c in loads:
        c.start()

    barrier = pltpu.get_barrier_semaphore()
    pl.semaphore_signal(barrier, inc=1, device_id=sibling, device_id_type=MESH)

    def greet(d, _):
        pl.semaphore_signal(barrier, inc=1, device_id=peer(d), device_id_type=MESH)
        return 0

    lax.fori_loop(1, 16, greet, 0)
    pl.semaphore_wait(barrier, 16)

    first = [
        send(a.at[:, 1 - core], t, sib_send.at[n], sib_recv.at[n], sibling)
        for n, (a, t) in enumerate(((f_ref, sf), (r_ref, sr), (u_ref, su), (coef_ref, sc)))
    ]
    for c in first:
        c.start()

    def prompt_copy(d):
        return send(p_ref, prompts.at[chip], p_send.at[d], p_recv.at[d], peer(d))

    lax.fori_loop(1, 16, lambda d, _: (prompt_copy(d).start(), 0)[1], 0)
    prompts[chip] = p_ref[...]

    unit = lambda u, _: (
        inside_unit(u, x_v, g_v, b_ref, c_ref, la_ref, w3_ref, s2_ref, inner_v, pt_v, dx_v), 0
    )[1]
    for c in loads:
        c.wait()
    lax.fori_loop(0, 8, unit, 0)

    for c in first:
        c.wait()
    is0 = core == 0
    pick = lambda mine, theirs: (jnp.where(is0, mine, theirs), jnp.where(is0, theirs, mine))

    def combine(q, _):
        split = split_of(2 * q + core)
        t0, t1 = pick(coef_ref[q, core], sc[q])
        f0, f1 = pick(f_ref[q, core], sf[q])
        r0, r1 = pick(r_ref[q, core], sr[q])
        comb[q, 0:CHUNK, :] = f1 + spread(t1, 0, split) * f0
        comb[q, CHUNK : 2 * CHUNK, :] = r0 + spread(t0, 2, split) * r1
        comb[q, 2 * CHUNK : 3 * CHUNK, :] = (
            u_ref[q, core] + su[q] + spread(t0, 3, split) * r1
        )
        comb[q, 3 * CHUNK :, :] = jnp.concatenate(
            [
                t0[0:2] * t1[0:2],
                t1[2:4] + t1[0:2] * t0[2:4],
                t0[4:6] * t1[4:6],
                t1[6:8] + t0[6:8] * t1[4:6],
            ],
            axis=0,
        )
        return 0

    lax.fori_loop(0, 16, combine, 0)

    def out_copy(d):
        to = peer(d)
        return send(comb.at[to[1] // 2], got.at[d], a_send.at[d], a_recv.at[d], to)

    lax.fori_loop(1, 16, lambda d, _: (out_copy(d).start(), 0)[1], 0)
    got[0] = comb[chip]

    lax.fori_loop(8, 34, unit, 0)

    lax.fori_loop(1, 16, lambda d, _: (out_copy(d).wait(), 0)[1], 0)
    split = split_of(seq)

    def slot(q):
        return ((y + 4 - q // 4) % 4) * 4 + (z + 4 - q % 4) % 4

    own = p_ref[...]

    def forward(q, e):
        s = slot(q)
        back[q, 0:CHUNK, :] = e
        t = got[s, 3 * CHUNK :, :]
        return spread(t, 0, split) * e + spread(t, 1, split) * own + got[s, 0:CHUNK, :]

    lax.fori_loop(0, 16, forward, jnp.zeros((CHUNK, 128), F32))

    def backward(n, carry):
        lv, total = carry
        q = 15 - n
        s = slot(q)
        back[q, CHUNK:, :] = lv
        t = got[s, 3 * CHUNK :, :]
        total = total + got[s, 2 * CHUNK : 3 * CHUNK, :] + spread(t, 3, split) * lv
        return spread(t, 2, split) * lv + got[s, CHUNK : 2 * CHUNK, :], total

    zero = jnp.zeros((CHUNK, 128), F32)
    _, total = lax.fori_loop(0, 16, backward, (zero, zero))
    pg_ref[...] = total

    def back_copy(d):
        to = peer(d)
        return send(back.at[to[1] // 2], ret.at[chip], b_send.at[d], b_recv.at[d], to)

    lax.fori_loop(1, 16, lambda d, _: (back_copy(d).start(), 0)[1], 0)
    ret[chip] = back[chip]

    lax.fori_loop(34, NBLK * PAIRS, unit, 0)
    for k in range(NBLK):
        keep = iota((BLOCK, BLOCK), 1) >= iota((BLOCK, BLOCK), 0)
        pt_ref[k] = jnp.where(keep, pt_v[k], 0.0).astype(BF16)
    store = pltpu.make_async_copy(dx_v, dx_hbm, load_sem.at[2])
    store.start()

    lax.fori_loop(1, 16, lambda d, _: (prompt_copy(d).wait(), 0)[1], 0)
    lax.fori_loop(1, 16, lambda d, _: (back_copy(d).wait(), 0)[1], 0)

    def finish(q, _):
        split = split_of(2 * q + core)
        t0, t1 = pick(coef_ref[q, core], sc[q])
        f0, _ = pick(f_ref[q, core], sf[q])
        _, r1 = pick(r_ref[q, core], sr[q])
        e0 = ret[q, 0:CHUNK, :]
        l1 = ret[q, CHUNK:, :]
        prompt = prompts[q]
        e1 = spread(t0, 0, split) * e0 + spread(t0, 1, split) * prompt + f0
        l0 = spread(t1, 2, split) * l1 + r1
        e_ref[q, core], sib_e[q] = pick(e0, e1)
        l_ref[q, core], sib_l[q] = pick(l0, l1)
        pr_ref[q, core] = prompt
        return 0

    lax.fori_loop(0, 16, finish, 0)
    last = [
        send(s, t.at[:, core], sib_send.at[4 + n], sib_recv.at[4 + n], sibling)
        for n, (s, t) in enumerate(((sib_e, e_ref), (sib_l, l_ref), (prompts, pr_ref)))
    ]
    for c in last:
        c.start()
    for c in last:
        c.wait()
    store.wait()


def carry(f, r, u, coef, p, x, g, b, c, la, w3, s2):
    v = pl.BlockSpec(memory_space=pltpu.VMEM)
    a = pl.BlockSpec(memory_space=pl.ANY)
    split = lambda s: s.reshape(16, 2, CHUNK, 128)
    st = jax.ShapeDtypeStruct((16, 2, CHUNK, 128), F32)
    half = pltpu.VMEM((16, CHUNK, 128), F32)
    dma = lambda n: pltpu.SemaphoreType.DMA((n,))
    return pl.pallas_call(
        carry_kernel,
        in_specs=[v] * 5 + [a, a] + [v] * 5,
        out_specs=[v] * 5 + [a],
        out_shape=[
            st, st, st, jax.ShapeDtypeStruct((CHUNK, 128), F32),
            jax.ShapeDtypeStruct((NBLK, BLOCK, BLOCK), BF16),
            jax.ShapeDtypeStruct((TOK, WIDTH), BF16),
        ],
        scratch_shapes=[
            pltpu.VMEM((TOK, WIDTH), BF16), pltpu.VMEM((TOK, WIDTH), BF16), pltpu.VMEM((TOK, WIDTH), BF16),
            pltpu.VMEM((BLOCK, BLOCK), F32), pltpu.VMEM((NBLK, BLOCK, BLOCK), F32),
            half, half, half, pltpu.VMEM((16, 8, 128), F32), half,
            pltpu.VMEM((16, MESSAGE, 128), F32), pltpu.VMEM((16, MESSAGE, 128), F32),
            pltpu.VMEM((16, 2 * CHUNK, 128), F32), pltpu.VMEM((16, 2 * CHUNK, 128), F32),
            half, half, half,
            dma(3), dma(7), dma(7), dma(16), dma(16), dma(16), dma(16), dma(16), dma(16),
        ],
        compiler_params=pltpu.CompilerParams(
            collective_id=0, has_side_effects=True, vmem_limit_bytes=VMEM_LIMIT
        ),
    )(split(f), split(r), split(u), coef.reshape(16, 2, 8, 128), p, x, g, b, c, la, w3, s2)


def gradient_kernel(
    lens_ref, x_ref, g_ref, dx_ref, e_ref, l_ref, p_ref, loc_ref,
    b_ref, c_ref, la_ref, s2_ref, x2_ref, g2_ref, pt_ref, out_ref, bc_ref, acc_ref,
):
    pair = pl.program_id(0)
    ns, nl = flags(lens_ref)

    @pl.when(pair == 0)
    def _():
        for k in range(NBLK):
            rows = slice(BLOCK * k, BLOCK * (k + 1))
            acc_ref[rows, :128] = dot(pt_ref[k], c_ref[rows, :])
            acc_ref[rows, 128:] = dot(pt_ref[k], b_ref[rows, :], TN)

    sel = selector(2 * pair, 2, 64, 128)
    wx = dot(x2_ref[...], sel)
    sx = (x_ref[...].astype(F32) * wx).astype(BF16)
    sg = (g_ref[...].astype(F32) * dot(g2_ref[...], sel)).astype(BF16)
    st = dot(s2_ref[...], sel)
    dec = pair_decays(la_ref, pair)
    prompt = p_ref[...]
    entering = []
    state = e_ref[...]
    for k in range(NBLK):
        state = state * ns[k] + prompt * (1.0 - ns[k])
        entering.append(state.astype(BF16))
        if k < NBLK - 1:
            state = dec[k] * state + loc_ref[k]
    leaving = [None] * NBLK
    state = l_ref[...]
    for k in reversed(range(NBLK)):
        state = state * nl[k]
        leaving[k] = state.astype(BF16)
        if k > 0:
            state = dec[k] * state + loc_ref[k + 1]
    for k in range(NBLK):
        rows = slice(BLOCK * k, BLOCK * (k + 1))
        outer = dot(b_ref[rows, :], leaving[k], NT)
        out_ref[rows, :] = (st[rows] * dx_ref[rows, :].astype(F32) + wx[rows] * outer).astype(BF16)
        acc_ref[rows, :128] += dot(sx[rows], leaving[k])
        acc_ref[rows, 128:] += dot(sg[rows], entering[k])

    @pl.when(pair == PAIRS - 1)
    def _():
        bc_ref[...] = acc_ref[...].astype(BF16)


def gradients(lens, x, g, dx, e, l, p, loc, b, c, la, s2, x2, g2, pt):
    whole = lambda *shape: pl.BlockSpec(shape, lambda i: (0,) * len(shape))
    lanes = pl.BlockSpec((TOK, 128), lambda i: (0, i))
    rows = pl.BlockSpec((128, 128), lambda i: (i, 0))
    flat = lambda s: s.reshape(WIDTH, STATE)
    cols = whole(TOK, 128)
    return pl.pallas_call(
        gradient_kernel,
        grid=(PAIRS,),
        in_specs=[
            pl.BlockSpec(memory_space=pltpu.SMEM), lanes, lanes, lanes, rows, rows, rows,
            pl.BlockSpec((4, 128, 128), lambda i: (0, i, 0)),
            cols, cols, whole(HEADS, TOK), cols, cols, cols, whole(NBLK, BLOCK, BLOCK),
        ],
        out_specs=[lanes, whole(TOK, 256)],
        out_shape=[
            jax.ShapeDtypeStruct((TOK, WIDTH), BF16), jax.ShapeDtypeStruct((TOK, 256), BF16)
        ],
        scratch_shapes=[pltpu.VMEM((TOK, 256), F32)],
        compiler_params=pltpu.CompilerParams(vmem_limit_bytes=VMEM_LIMIT),
    )(lens, x, g, dx, flat(e), flat(l), flat(p), loc, b, c, la, s2, x2, g2, pt)


SLABS = 8
SLAB = DMODEL // SLABS
ROWS = ((0, 16), (16, 32), (32, 40))


def weight_kernel(
    li_hbm, bc_ref, out_ref,
    li_v, part, sib, h,
    r1a, r1b, r1c, s1a, s1b, s1c, r2a, r2b, r2c, s2a, s2b, s2c, r3a, r3b, r3c,
    load_sem, sib_send, sib_recv, sends, recvs,
):
    x, seq = lax.axis_index("group"), lax.axis_index("seq")
    core = seq % 2
    y, z = seq // 8, (seq // 2) % 4
    sibling = (x, seq + 1 - 2 * core)

    def index(yy, zz):
        return (yy * 4 + zz) * 2 + core

    def to_x(d):
        return ((x + d) % 4, seq)

    def to_y(d):
        return (x, index((y + d) % 4, z))

    def to_z(d):
        return (x, index(y, (z + d) % 4))

    def load(m):
        return pltpu.make_async_copy(
            li_hbm.at[:, SLAB * m : SLAB * (m + 1)], li_v.at[m], load_sem.at[m]
        )

    for m in range(SLABS):
        load(m).start()
    barrier = pltpu.get_barrier_semaphore()
    targets = [sibling] + [to(d) for to in (to_x, to_y, to_z) for d in (1, 2, 3)]
    for t in targets:
        pl.semaphore_signal(barrier, inc=1, device_id=t, device_id_type=MESH)
    pl.semaphore_wait(barrier, len(targets))

    def sib_copy(m):
        return pltpu.make_async_remote_copy(
            src_ref=part.at[m, :, 1 - core], dst_ref=sib.at[m],
            send_sem=sib_send.at[m], recv_sem=sib_recv.at[m],
            device_id=sibling, device_id_type=MESH,
        )

    bc = bc_ref[...]
    for m in range(SLABS):
        load(m).wait()
        part[m] = dot(li_v[m], bc, TN).reshape(8, 2, 40, 256)
        sib_copy(m).start()
    for m in range(SLABS):
        sib_copy(m).wait()
        h[m // 2, 2 * (m % 2) : 2 * (m % 2) + 2] = (part[m, :, core] + sib[m]).reshape(2, 4, 40, 256)

    def copy(n, stage, d, src, dst, to):
        return pltpu.make_async_remote_copy(
            src_ref=src, dst_ref=dst, send_sem=sends.at[n, stage, d], recv_sem=recvs.at[n, stage, d],
            device_id=to, device_id_type=MESH,
        )

    me = lambda v, d: (v + d) % 4

    def first(n, d):
        lo, hi = ROWS[n]
        size = hi - lo
        rows = pl.ds(lo, size)
        if n == 0:
            return copy(n, 0, d, h.at[me(x, d), :, :, rows], r1a.at[d], to_x(d))
        if n == 1:
            return copy(n, 0, d, h.at[:, me(y, d), :, rows], r1b.at[d], to_y(d))
        return copy(n, 0, d, h.at[:, :, me(z, d), rows], r1c.at[d], to_z(d))

    def second(n, d):
        if n == 0:
            return copy(n, 1, d, s1a.at[me(y, d)], r2a.at[d], to_y(d))
        if n == 1:
            return copy(n, 1, d, s1b.at[:, me(z, d)], r2b.at[d], to_z(d))
        return copy(n, 1, d, s1c.at[me(x, d)], r2c.at[d], to_x(d))

    def third(n, d):
        if n == 0:
            return copy(n, 2, d, s2a.at[me(z, d)], r3a.at[d], to_z(d))
        if n == 1:
            return copy(n, 2, d, s2b.at[me(x, d)], r3b.at[d], to_x(d))
        return copy(n, 2, d, s2c.at[me(y, d)], r3c.at[d], to_y(d))

    each = [(n, d) for d in (1, 3, 2) for n in range(3)]
    for n, d in each:
        first(n, d).start()
    for n in range(3):
        for d in (1, 2, 3):
            first(n, d).wait()
        if n == 0:
            s1a[...] = h[x, :, :, 0:16] + r1a[1] + r1a[2] + r1a[3]
        elif n == 1:
            s1b[...] = h[:, y, :, 16:32] + r1b[1] + r1b[2] + r1b[3]
        else:
            s1c[...] = h[:, :, z, 32:40] + r1c[1] + r1c[2] + r1c[3]
        for d in (1, 3, 2):
            second(n, d).start()
    for n in range(3):
        for d in (1, 2, 3):
            second(n, d).wait()
        if n == 0:
            s2a[...] = s1a[y] + r2a[1] + r2a[2] + r2a[3]
        elif n == 1:
            s2b[...] = s1b[:, z] + r2b[1] + r2b[2] + r2b[3]
        else:
            s2c[...] = s1c[x] + r2c[1] + r2c[2] + r2c[3]
        for d in (1, 3, 2):
            third(n, d).start()
    for n, (mine, r, at) in enumerate(((s2a, r3a, z), (s2b, r3b, x), (s2c, r3c, y))):
        for d in (1, 2, 3):
            third(n, d).wait()
        out_ref[ROWS[n][0] : ROWS[n][1], :] = mine[at] + r[1] + r[2] + r[3]


def weight_gradient(li, bc):
    v = lambda *shape: pltpu.VMEM(shape, F32)
    dma = lambda *n: pltpu.SemaphoreType.DMA(n)
    return pl.pallas_call(
        weight_kernel,
        in_specs=[pl.BlockSpec(memory_space=pl.ANY), pl.BlockSpec(memory_space=pltpu.VMEM)],
        out_specs=pl.BlockSpec(memory_space=pltpu.VMEM),
        out_shape=jax.ShapeDtypeStruct((40, 256), F32),
        scratch_shapes=[
            pltpu.VMEM((SLABS, TOK, SLAB), BF16),
            v(SLABS, 8, 2, 40, 256), v(SLABS, 8, 40, 256), v(4, 4, 4, 40, 256),
            v(4, 4, 4, 16, 256), v(4, 4, 4, 16, 256), v(4, 4, 4, 8, 256),
            v(4, 4, 16, 256), v(4, 4, 16, 256), v(4, 4, 8, 256),
            v(4, 4, 16, 256), v(4, 4, 16, 256), v(4, 4, 8, 256),
            v(4, 16, 256), v(4, 16, 256), v(4, 8, 256),
            v(4, 16, 256), v(4, 16, 256), v(4, 8, 256),
            dma(SLABS), dma(SLABS), dma(SLABS), dma(3, 3, 4), dma(3, 3, 4),
        ],
        compiler_params=pltpu.CompilerParams(
            collective_id=1, has_side_effects=True, vmem_limit_bytes=VMEM_LIMIT
        ),
    )(li, bc)


def body(li, x, g, b, c, step, rates, prompt, lens):
    li, x, g, b, c, step, prompt = li[0], x[0], g[0], b[0], c[0], step[0], prompt[0]
    f, r, u, loc, coef, la, w3, s2, x2, g2 = summarize(lens, step, rates.reshape(HEADS, 1), x, g, b, c)
    e, l, p, prompt_grad, pt, dx = carry(f, r, u, coef, prompt, x, g, b, c, la, w3, s2)
    x_grad, bc = gradients(lens, x, g, dx, e, l, p, loc, b, c, la, s2, x2, g2, pt)
    weight_grad = weight_gradient(li, bc)
    return x_grad[None], prompt_grad[None], weight_grad


def solution(mesh):
    in_specs = (
        P("group", "seq", None),
        P("group", "seq", None),
        P("group", "seq", None),
        P("group", "seq", None),
        P("group", "seq", None),
        P("group", None, "seq"),
        P(),
        P("group", "seq", None),
        P("group", None),
    )
    out_specs = (P("group", "seq", None), P("group", "seq", None), P(("group", "seq"), None))
    return jax.shard_map(body, mesh=mesh, in_specs=in_specs, out_specs=out_specs, check_vma=False)
```

time: 1170 us -> 155 us (0.13)
  waiting for transfers between devices: 645 us -> 0 us
  other arithmetic: 169 us -> 0 us
  Pallas kernels: 0 us -> 150 us
  local copies, waits for them, and re-layouts: 136 us -> 3.37 us
  blocking collectives: 132 us -> 0 us
  matrix products: 65.1 us -> 0 us
  between operations: 14.7 us -> 0.67 us
    unnamed x6 -> x0, waiting for transfers between devices: 622 us -> none
    pallas_call x0 -> x4, Pallas kernels: none -> 150 us  [the longest x1 71.8 us: carry(): pl.pallas_call(carry_kernel, in_specs=[v] * 5 + [a, a] + [v] * 5, out_spe...]
    unnamed x1 -> x0, blocking collectives: 132 us -> none
    select_n x65 -> x0, other arithmetic: 105 us -> none  [the longest x64 105 us: step(): return jax.tree.map(lambda a, b: jnp.where(reached, a, b), new, before)]
    dot_general x31 -> x0, matrix products: 65.1 us -> none  [the longest x3 14.3 us: process(): jnp.einsum('thp,shp->hts', grad_block, x_block, preferred_element_type=jn...]
    another operation x18 -> x0, local copies, waits for them, and re-layouts: 36.5 us -> none
    dynamic_update_slice x12 -> x0, other arithmetic: 32.9 us -> none  [body(): lax.map(lambda items: summarize(*items, decay_rates), (x_blocks, grad_blo...]
    unnamed x39 -> x4, local copies, waits for them, and re-layouts: 34.8 us -> 2.02 us
  transfers between devices with their start and end apart: 5 -> 0, of which waited for: 2 -> 0; matrix products, arithmetic and copies ran while one was open for 31% -> 0% of each run, Pallas kernels for 0% -> 0%
where the time goes in v1:
time: 155 us; the launch traced here: 154 us
  Pallas kernels  150 us (97%)
  local copies, waits for them, and re-layouts  3.37 us (2%)
    pallas_call x1, Pallas kernels, carry(): pl.pallas_call(carry_kernel, in_specs=[v] * 5 + [a, a] + [v] * 5, out_spe...  71.8 us
    pallas_call x1, Pallas kernels, weight_gradient(): pl.pallas_call(weight_kernel, in_specs=[pl.BlockSpec(memory_space=pl.ANY)...  35.8 us
    pallas_call x1, Pallas kernels, gradients(): pl.pallas_call(gradient_kernel, grid=(PAIRS,), in_specs=[pl.BlockSpec(mem...  21.9 us
    pallas_call x1, Pallas kernels, summarize(): pl.pallas_call(summary_kernel, grid=(PAIRS,), in_specs=[pl.BlockSpec(memo...  20.5 us

profile of v1, /device:TPU:0, one launch (start us, length us, event | category | flops | bytes accessed | tf_op | source)
XLA Modules:
  0.0 154.1 jit_solution(12689105054927448850)
XLA Ops:
  0.6 1.3 copy.12.rate_ref
  2.0 20.5 %shard_map.112 = (f32[2560,128]{1,0:T(8,128)}, f32[2560,128]{1,0:T(8,128)}, f32[2560,128]{1,0:T(8,128)}, f32[4,2560,128]{2,1,0:T(8,128)}, f32[32,8,128]{2,1,0:T(...) custom-call(s32[1,4]{1,0:T(1,128)} %lens_ref.3, ...), custom_call_target="tpu_custom_call" | custom-call | tf_op jit(solution)/shard_map/pallas_call | solution.py:162
  22.5 71.8 %shard_map.113 = (f32[16,2,80,128]{3,2,1,0:T(8,128)}, f32[16,2,80,128]{3,2,1,0:T(8,128)}, f32[16,2,80,128]{3,2,1,0:T(8,128)}, f32[80,128]{1,0:T(8,128)}, bf16[3,...) custom-call(f32[16,2,80,128]{3,2,1,0:T(8,128)} %bitcast.30, f32[16,2,80,128]{3,2,1,0:T(8,128)} %bitcast.31, ...), custom_call_target="tpu_custom_call" | custom-call | tf_op jit(solution)/shard_map/pallas_call | solution.py:407
  94.3 21.9 %shard_map.114 = (bf16[768,2560]{1,0:T(8,128)(2,1)}, bf16[768,256]{1,0:T(8,128)(2,1)}) custom-call(s32[1,4]{1,0:T(1,128)} %lens_ref.3, bf16[768,2560]{1,0:T(8,128)(2,1)} %bitcast.19, bf16[768,2560]{1,0:T(8,128)(2,1)} %bitcast.22, bf16[768,2560]{1,0:T(8,128)(2,1)} %get-tuple-element.28.dx_ref, f32[2560,128]{1,0:T(8,128)} %bitcast.33, f32[2560,128]{1,0:T(8,128)} %bitcast.34, ...), custom_call_target="tpu_custom_call" | custom-call | tf_op jit(solution)/shard_map/pallas_call | solution.py:484
  116.2 0.0 copy-start
  116.2 35.8 %shard_map.115 = f32[40,256]{1,0:T(8,128)} custom-call(bf16[768,5120]{1,0:T(8,128)(2,1)} %bitcast.23, bf16[768,256]{1,0:T(8,128)(2,1)} %get-tuple-element.38.bc_ref), custom_call_target="tpu_custom_call" | custom-call | tf_op jit(solution)/shard_map/pallas_call | solution.py:624
  152.1 0.0 copy-done
  152.1 0.6 copy.15
  152.7 1.4 copy.16
Async XLA Ops:
  116.2 35.8 %copy-start = (f32[80,128]{1,0:T(8,128)S(1)}, f32[80,128]{1,0:T(8,128)}, u32[]{:S(2)}) copy-start(f32[80,128]{1,0:T(8,128)} %get-tuple-element.37) | copy-start | bytes 122884

commit v2 on v0

v2 whole, which is shorter than its diff:
```python
from functools import partial

import jax
import jax.numpy as jnp
from jax import lax
from jax.experimental import pallas as pl
from jax.experimental.pallas import tpu as pltpu
from jax.sharding import PartitionSpec as P

BLOCK = 256
NBLK = 3
TOK = BLOCK * NBLK
HEADS = 40
STATE = 128
WIDTH = 2560
DMODEL = 5120
PHASES = 5
PHEADS = HEADS // PHASES
PLANES = PHEADS * 64
PPAIRS = PHEADS // 2
PUNITS = NBLK * PPAIRS
F32 = jnp.float32
BF16 = jnp.bfloat16
MESH = pl.DeviceIdType.MESH
NN = (((1,), (0,)), ((), ()))
TN = (((0,), (0,)), ((), ()))
NT = (((1,), (1,)), ((), ()))
LOG2E = 1.4426950408889634
VMEM_LIMIT = 60 * 1024 * 1024


def dot(a, b, dims=NN):
    return lax.dot_general(a, b, dims, preferred_element_type=F32)


def iota(shape, dim):
    return lax.broadcasted_iota(jnp.int32, shape, dim)


def flags(lens_ref):
    first = lax.axis_index("seq") * NBLK
    e1 = lens_ref[0, 0]
    e2 = e1 + lens_ref[0, 1]
    e3 = e2 + lens_ref[0, 2]
    e4 = e3 + lens_ref[0, 3]
    not_start, not_last = [], []
    for k in range(NBLK):
        at = first + k
        start = (at == 0) | (at == e1) | (at == e2) | (at == e3)
        last = (at == e1 - 1) | (at == e2 - 1) | (at == e3 - 1) | (at == e4 - 1)
        not_start.append(jnp.where(start, 0.0, 1.0).astype(F32))
        not_last.append(jnp.where(last, 0.0, 1.0).astype(F32))
    return not_start, not_last


def blockrows(k):
    return slice(BLOCK * k, BLOCK * (k + 1))


def gather(table, index):
    return jnp.take_along_axis(table, index, axis=1)


def half_heads(pair, rows):
    return 2 * pair + iota((rows, 128), 1) // 64


def prepare(step_ref, rate_ref, b_ref, c_ref, la_v, t1_v, t2_v, inner_v, pt_v, acc_v):
    step = step_ref[...]
    same = iota((HEADS, HEADS), 0) == iota((HEADS, HEADS), 1)
    spread = jnp.broadcast_to(rate_ref[...], (HEADS, HEADS))
    rate = jnp.sum(jnp.where(same, spread, 0.0), axis=1, keepdims=True)
    la = -step * rate
    place = iota((HEADS, TOK), 1) % BLOCK
    shift = 1
    while shift < BLOCK:
        la = la + jnp.where(place >= shift, pltpu.roll(la, shift, 1), 0.0)
        shift *= 2
    la = la * LOG2E
    la_v[...] = la
    ends = [la[:, BLOCK * (k + 1) - 1 : BLOCK * (k + 1)] for k in range(NBLK)]
    end = jnp.concatenate([jnp.broadcast_to(e, (HEADS, BLOCK)) for e in ends], axis=1)
    empty = jnp.zeros((8, TOK), F32)
    t1_v[...] = jnp.concatenate([la, step, jnp.exp2(end - la) * step, empty], axis=0).T
    t2_v[...] = jnp.concatenate([jnp.exp2(la), jnp.zeros((88, TOK), F32)], axis=0).T
    keep = iota((BLOCK, BLOCK), 1) >= iota((BLOCK, BLOCK), 0)
    for k in range(NBLK):
        inner_v[k] = jnp.where(keep, dot(b_ref[blockrows(k), :], c_ref[blockrows(k), :], NT), 0.0)
        pt_v[k] = jnp.zeros((BLOCK, BLOCK), F32)
    acc_v[...] = jnp.zeros_like(acc_v)


def phase_decays(la_v, j):
    la = la_v[pl.ds(pl.multiple_of(PHEADS * j, PHEADS), PHEADS), :]
    out = []
    for k in range(NBLK):
        at = BLOCK * (k + 1) - 1
        out.append(jnp.broadcast_to(jnp.exp2(la[:, at : at + 1]), (PHEADS, 128))[:, None, :])
    return out


def summarize(j, ns, nl, x_v, g_v, b_ref, c_ref, la_v, t1_v, t2_v, sx_v, sg_v, loc_v, mine):
    ls, lg = [], []
    for k in range(NBLK):
        rows = blockrows(k)
        sx, sg = [], []
        for p in range(PPAIRS):
            lanes = pl.ds(pl.multiple_of(PLANES * j + 128 * p, 128), 128)
            heads = half_heads(PPAIRS * j + p, BLOCK)
            sx.append((x_v[rows, lanes].astype(F32) * gather(t1_v[rows, :], heads + 2 * HEADS)).astype(BF16))
            sg.append((g_v[rows, lanes].astype(F32) * gather(t2_v[rows, :], heads)).astype(BF16))
            sx_v[rows, lanes] = sx[p]
            sg_v[rows, lanes] = sg[p]
        ls.append(dot(jnp.concatenate(sx, axis=1), b_ref[rows, :], TN).reshape(PHEADS, 64, 128))
        lg.append(dot(jnp.concatenate(sg, axis=1), c_ref[rows, :], TN).reshape(PHEADS, 64, 128))
    for n, value in enumerate((ls[0], ls[1], lg[0], lg[1], lg[2])):
        loc_v[j, n] = value
    dec = phase_decays(la_v, j)
    f = ls[0]
    for k in range(1, NBLK):
        f = (dec[k] * ns[k]) * f + ls[k]
    r = lg[2]
    for k in (1, 0):
        r = (dec[k] * nl[k]) * r + lg[k]
    mine[j, :, :, 0:16, :] = f.reshape(16, 2, 16, 128)
    mine[j, :, :, 16:32, :] = r.reshape(16, 2, 16, 128)
    af = ab = jnp.ones((PHEADS, 1, 128), F32)
    pc = jnp.zeros((PHEADS, 1, 128), F32)
    for k in range(NBLK):
        af = af * (dec[k] * ns[k])
        pc = dec[k] * (pc * ns[k] + (1.0 - ns[k]))
        ab = ab * (dec[k] * nl[k])
    empty = jnp.zeros((5, 128), F32)
    for h in range(PHEADS):
        tile = jnp.concatenate([af[h], pc[h], ab[h], empty], axis=0)
        for q in (2 * h, 2 * h + 1):
            for c in range(2):
                mine[j, q, c, 32:40, :] = tile


def inside_unit(u, x_v, g_v, la_v, t1_v, inner_v, pt_v, dx_v):
    j, v = u // PUNITS, u % PUNITS
    k, pair = v // PPAIRS, PPAIRS * j + v % PPAIRS
    r = pl.ds(pl.multiple_of(k * BLOCK, BLOCK), BLOCK)
    l = pl.ds(pl.multiple_of(pair * 128, 128), 128)
    g = g_v[r, l]
    table = t1_v[r, :]
    xs = (x_v[r, l].astype(F32) * gather(table, half_heads(pair, BLOCK) + HEADS)).astype(BF16)
    lane = iota((1, 128), 1)
    masks = [jnp.where((lane >= 64) == bool(n), 1.0, 0.0).astype(BF16) for n in range(2)]
    gs = [g * m for m in masks]
    low = jnp.concatenate([gs[0][128:], gs[1][128:]], axis=0)
    p0 = dot(jnp.concatenate([xs[:128] * masks[0], xs[:128] * masks[1]], axis=0), g, NT)
    p1 = dot(xs[128:], low, NT)
    a00, a01, a11, w11, d0 = [], [], [], [], []
    for n in range(2):
        row = la_v[pl.ds(2 * pair + n, 1), r]
        col = gather(table, jnp.full((BLOCK, 128), 2 * pair + n, jnp.int32))
        pn = p0[128 * n : 128 * (n + 1)]
        q00 = jnp.exp2(jnp.minimum(row[:, :128] - col[:128], 0.0))
        q01 = jnp.exp2(jnp.minimum(row[:, 128:] - col[:128], 0.0))
        q11 = jnp.exp2(jnp.minimum(row[:, 128:] - col[128:], 0.0))
        a00.append(q00 * pn[:, :128])
        a01.append(q01 * pn[:, 128:])
        a11.append(q11 * p1[:, 128 * n : 128 * (n + 1)])
        w00 = (q00 * inner_v[k, :128, :128]).astype(BF16)
        w01 = (q01 * inner_v[k, :128, 128:]).astype(BF16)
        w11.append((q11 * inner_v[k, 128:, 128:]).astype(BF16))
        d0.append(dot(jnp.concatenate([w00, w01], axis=1), gs[n]))
    pt_v[k, :128, :128] += a00[0] + a00[1]
    pt_v[k, :128, 128:] += a01[0] + a01[1]
    pt_v[k, 128:, 128:] += a11[0] + a11[1]
    d1 = dot(jnp.concatenate(w11, axis=1), low)
    dx_v[r, l] = jnp.concatenate([d0[0] + d0[1], d1], axis=0).astype(BF16)


def gradients(j, ns, nl, b_ref, la_v, t1_v, sx_v, sg_v, loc_v, prompt, el_v, dx_v, acc_v, pterm_ref):
    dec = phase_decays(la_v, j)
    el = el_v[j]
    shape = (PHEADS, 64, 128)
    prompt = prompt.reshape(shape)
    state = el[:, :, 0:16].reshape(shape)
    entering = []
    for k in range(NBLK):
        state = state * ns[k] + prompt * (1.0 - ns[k])
        entering.append(state.reshape(PLANES, 128).astype(BF16))
        if k < NBLK - 1:
            state = dec[k] * state + loc_v[j, k]
    state = el[:, :, 16:32].reshape(shape)
    leaving = [None] * NBLK
    total = None
    for k in reversed(range(NBLK)):
        state = state * nl[k]
        leaving[k] = state.reshape(PLANES, 128).astype(BF16)
        state = dec[k] * state + loc_v[j, 2 + k]
        at_start = state * (1.0 - ns[k])
        total = at_start if total is None else total + at_start
    pterm_ref[j] = total
    lanes = pl.ds(pl.multiple_of(PLANES * j, PLANES), PLANES)
    for k in range(NBLK):
        rows = blockrows(k)
        outer = dot(b_ref[rows, :], leaving[k], NT)
        table = t1_v[rows, :]
        for p in range(PPAIRS):
            at = pl.ds(pl.multiple_of(PLANES * j + 128 * p, 128), 128)
            heads = half_heads(PPAIRS * j + p, BLOCK)
            near = gather(table, heads + HEADS) * dx_v[rows, at].astype(F32)
            far = gather(table, heads + 2 * HEADS) * outer[:, 128 * p : 128 * (p + 1)]
            dx_v[rows, at] = (near + far).astype(BF16)
        acc_v[rows, :128] += dot(sx_v[rows, lanes], leaving[k])
        acc_v[rows, 128:] += dot(sg_v[rows, lanes], entering[k])


TICKS = PHASES + 6
STEP_UNITS = 3


def scan_kernel(
    lens_ref, step_ref, rate_ref, x_hbm, g_hbm, b_ref, c_ref, p_ref,
    xg_hbm, bc_ref, pterm_ref,
    x_v, g_v, dx_v, sx_v, sg_v, la_v, t1_v, t2_v, inner_v, pt_v, acc_v, loc_v,
    mine, sib_in, comb, got, back, ret, sib_out, el_v, prompts,
    x_sem, g_sem, o_sem, f_send, f_recv, l_send, l_recv, p_send, p_recv, a_send, a_recv, b_send, b_recv,
):
    group, seq = lax.axis_index("group"), lax.axis_index("seq")
    core = seq % 2
    chip = seq // 2
    y, z = chip // 4, chip % 4
    sibling = (group, chip * 2 + (1 - core))
    is0 = core == 0

    def chip_at(d):
        return ((y + d // 4) % 4) * 4 + (z + d % 4) % 4

    def send(src, dst, s, r, to):
        return pltpu.make_async_remote_copy(
            src_ref=src, dst_ref=dst, send_sem=s, recv_sem=r, device_id=to, device_id_type=MESH
        )

    def lanes(j):
        return pl.ds(pl.multiple_of(PLANES * j, PLANES), PLANES)

    def load_x(j):
        return pltpu.make_async_copy(x_hbm.at[:, lanes(j)], x_v.at[:, lanes(j)], x_sem.at[j])

    def load_g(j):
        return pltpu.make_async_copy(g_hbm.at[:, lanes(j)], g_v.at[:, lanes(j)], g_sem.at[j])

    def store(j):
        return pltpu.make_async_copy(dx_v.at[:, lanes(j)], xg_hbm.at[:, lanes(j)], o_sem.at[j])

    def each(lo, hi, f):
        def step(i, _):
            f(i)
            return 0

        lax.fori_loop(lo, hi, step, 0)

    def begin(j):
        load_x(j).start()
        load_g(j).start()

    each(0, PHASES, begin)

    barrier = pltpu.get_barrier_semaphore()
    pl.semaphore_signal(barrier, inc=1, device_id=sibling, device_id_type=MESH)
    each(1, 16, lambda d: pl.semaphore_signal(
        barrier, inc=1, device_id=(group, chip_at(d) * 2 + core), device_id_type=MESH
    ))
    pl.semaphore_wait(barrier, 16)

    def prompt_copy(d):
        return send(p_ref, prompts.at[chip, core], p_send.at[d], p_recv.at[d], (group, chip_at(d) * 2 + core))

    def prompt_pass():
        half = prompts.at[:, core]
        return send(half, half, p_send.at[0], p_recv.at[0], sibling)

    def chip_copy(j):
        return send(mine.at[j, :, 1 - core], sib_in.at[j], f_send.at[j], f_recv.at[j], sibling)

    def out_copy(j, d):
        to = chip_at(d)
        return send(comb.at[j, to], got.at[j, d], a_send.at[j, d], a_recv.at[j, d], (group, to * 2 + core))

    def back_copy(j, d):
        to = chip_at(d)
        return send(back.at[j, to], ret.at[j, chip], b_send.at[j, d], b_recv.at[j, d], (group, to * 2 + core))

    def last_copy(j):
        return send(sib_out.at[j], el_v.at[j, :, core], l_send.at[j], l_recv.at[j], sibling)

    each(1, 16, lambda d: prompt_copy(d).start())
    prompts[chip, core] = p_ref[...]

    prepare(step_ref, rate_ref, b_ref, c_ref, la_v, t1_v, t2_v, inner_v, pt_v, acc_v)
    ns, nl = flags(lens_ref)

    def pick(a, b):
        return jnp.where(is0, a, b), jnp.where(is0, b, a)

    def both(j):
        return pick(mine[j, :, core], sib_in[j])

    def combine(j):
        a, b = both(j)
        af0, pc0, ab0 = a[:, 32:33], a[:, 33:34], a[:, 34:35]
        af1, pc1, ab1 = b[:, 32:33], b[:, 33:34], b[:, 34:35]
        comb[j, :, 0:16, :] = b[:, 0:16] + af1 * a[:, 0:16]
        comb[j, :, 16:32, :] = a[:, 16:32] + ab0 * b[:, 16:32]
        comb[j, :, 32:40, :] = jnp.concatenate(
            [af0 * af1, pc1 + af1 * pc0, ab0 * ab1, jnp.zeros((16, 5, 128), F32)], axis=1
        )

    def prompt_rows(j, owner):
        at = 32 * j + owner
        return prompts[at // 10, (at // 5) % 2, pl.ds(pl.multiple_of(16 * (at % 5), 16), 16), :]

    def slot(q):
        return ((y + 4 - q // 4) % 4) * 4 + (z + 4 - q % 4) % 4

    def scan(j):
        own = prompt_rows(j, seq)
        e = jnp.zeros((16, 128), F32)
        for q in range(16):
            s = slot(q)
            back[j, q, 0:16, :] = e
            e = got[j, s, 32:33, :] * e + (got[j, s, 33:34, :] * own + got[j, s, 0:16, :])
        lv = jnp.zeros((16, 128), F32)
        for q in reversed(range(16)):
            s = slot(q)
            back[j, q, 16:32, :] = lv
            lv = got[j, s, 34:35, :] * lv + got[j, s, 16:32, :]

    def finish(j):
        a, b = both(j)
        e0, l1 = ret[j, :, 0:16, :], ret[j, :, 16:32, :]
        prompt = jnp.stack([prompt_rows(j, 2 * q + core) for q in range(16)], axis=0)
        e1 = a[:, 32:33] * e0 + (a[:, 33:34] * prompt + a[:, 0:16])
        l0 = b[:, 34:35] * l1 + b[:, 16:32]
        e_mine, e_other = pick(e0, e1)
        l_mine, l_other = pick(l0, l1)
        el_v[j, :, core, 0:16, :] = e_mine
        el_v[j, :, core, 16:32, :] = l_mine
        sib_out[j, :, 0:16, :] = e_other
        sib_out[j, :, 16:32, :] = l_other

    def units(lo):
        each(lo, lo + STEP_UNITS, lambda u: inside_unit(
            u, x_v, g_v, la_v, t1_v, inner_v, pt_v, dx_v
        ))

    def tick(t):
        @pl.when(t < PHASES)
        def _():
            load_x(t).wait()
            load_g(t).wait()
            summarize(t, ns, nl, x_v, g_v, b_ref, c_ref, la_v, t1_v, t2_v, sx_v, sg_v, loc_v, mine)
            chip_copy(t).start()

        @pl.when(t == 0)
        def _():
            each(1, 16, lambda d: prompt_copy(d).wait())
            prompt_pass().start()

        @pl.when((t >= 1) & (t < PHASES + 1))
        def _():
            j = t - 1
            chip_copy(j).wait()
            combine(j)
            each(1, 16, lambda d: out_copy(j, d).start())
            got[j, 0] = comb[j, chip]

        @pl.when(t < 10)
        def _():
            units(2 * STEP_UNITS * t)

        @pl.when(t == 2)
        def _():
            prompt_pass().wait()

        @pl.when((t >= 3) & (t < PHASES + 3))
        def _():
            j = t - 3
            each(1, 16, lambda d: out_copy(j, d).wait())
            scan(j)
            each(1, 16, lambda d: back_copy(j, d).start())
            ret[j, chip] = back[j, chip]

        @pl.when(t < 10)
        def _():
            units(2 * STEP_UNITS * t + STEP_UNITS)

        @pl.when((t >= 5) & (t < PHASES + 5))
        def _():
            j = t - 5
            each(1, 16, lambda d: back_copy(j, d).wait())
            finish(j)
            last_copy(j).start()

        @pl.when(t >= 6)
        def _():
            j = t - 6
            last_copy(j).wait()
            prompt = jnp.stack([prompt_rows(j, o) for o in range(32)], axis=0)
            gradients(j, ns, nl, b_ref, la_v, t1_v, sx_v, sg_v, loc_v, prompt, el_v, dx_v, acc_v, pterm_ref)
            store(j).start()

    each(0, TICKS, tick)

    keep = iota((BLOCK, BLOCK), 1) >= iota((BLOCK, BLOCK), 0)
    for k in range(NBLK):
        rows = blockrows(k)
        pt = jnp.where(keep, pt_v[k], 0.0).astype(BF16)
        bc_ref[rows, :128] = (acc_v[rows, :128] + dot(pt, c_ref[rows, :])).astype(BF16)
        bc_ref[rows, 128:] = (acc_v[rows, 128:] + dot(pt, b_ref[rows, :], TN)).astype(BF16)
    each(0, PHASES, lambda j: store(j).wait())


def scans(lens, step, rates, x, g, b, c, p):
    v = pl.BlockSpec(memory_space=pltpu.VMEM)
    a = pl.BlockSpec(memory_space=pl.ANY)
    wide = pltpu.VMEM((TOK, WIDTH), BF16)
    square = pltpu.VMEM((NBLK, BLOCK, BLOCK), F32)
    f = lambda *shape: pltpu.VMEM(shape, F32)
    dma = lambda *n: pltpu.SemaphoreType.DMA(n)
    return pl.pallas_call(
        scan_kernel,
        in_specs=[pl.BlockSpec(memory_space=pltpu.SMEM), v, v, a, a, v, v, v],
        out_specs=[a, v, v],
        out_shape=[
            jax.ShapeDtypeStruct((TOK, WIDTH), BF16),
            jax.ShapeDtypeStruct((TOK, 256), BF16),
            jax.ShapeDtypeStruct((PHASES, PHEADS, 64, 128), F32),
        ],
        scratch_shapes=[
            wide, wide, wide, wide, wide,
            f(HEADS, TOK), f(TOK, 128), f(TOK, 128), square, square, f(TOK, 256),
            f(PHASES, 5, PHEADS, 64, 128),
            f(PHASES, 16, 2, 40, 128), f(PHASES, 16, 40, 128), f(PHASES, 16, 40, 128), f(PHASES, 16, 40, 128),
            f(PHASES, 16, 32, 128), f(PHASES, 16, 32, 128), f(PHASES, 16, 32, 128),
            f(PHASES, 16, 2, 32, 128), f(16, 2, 80, 128),
            dma(PHASES), dma(PHASES), dma(PHASES), dma(PHASES), dma(PHASES), dma(PHASES), dma(PHASES),
            dma(16), dma(16), dma(PHASES, 16), dma(PHASES, 16), dma(PHASES, 16), dma(PHASES, 16),
        ],
        compiler_params=pltpu.CompilerParams(
            collective_id=0, has_side_effects=True, vmem_limit_bytes=VMEM_LIMIT
        ),
    )(lens, step, rates, x, g, b, c, p)


SLABS = 8
SLAB = DMODEL // SLABS
ROWS = ((0, 16), (16, 40), (16, 40))
COLS = ((0, 256), (0, 128), (128, 256))


def weight_kernel(
    li_hbm, bc_ref, pt_ref, out_ref, pg_ref,
    li_v, part, sib, h, sib_p, hp, pr1a, pr1b, ps1a, ps1b, pr2a, pr2b,
    r1a, r1b, r1c, s1a, s1b, s1c, r2a, r2b, r2c, s2a, s2b, s2c, r3a, r3b, r3c,
    load_sem, sib_send, sib_recv, sends, recvs, p_sends, p_recvs,
):
    x, seq = lax.axis_index("group"), lax.axis_index("seq")
    core = seq % 2
    y, z = seq // 8, (seq // 2) % 4
    sibling = (x, seq + 1 - 2 * core)

    def index(yy, zz):
        return (yy * 4 + zz) * 2 + core

    def to_x(d):
        return ((x + d) % 4, seq)

    def to_y(d):
        return (x, index((y + d) % 4, z))

    def to_z(d):
        return (x, index(y, (z + d) % 4))

    def load(m):
        return pltpu.make_async_copy(
            li_hbm.at[:, SLAB * m : SLAB * (m + 1)], li_v.at[m], load_sem.at[m]
        )

    for m in range(SLABS):
        load(m).start()
    barrier = pltpu.get_barrier_semaphore()
    targets = [sibling] + [to(d) for to in (to_x, to_y, to_z) for d in (1, 2, 3)]
    for t in targets:
        pl.semaphore_signal(barrier, inc=1, device_id=t, device_id_type=MESH)
    pl.semaphore_wait(barrier, len(targets))

    def sib_copy(m):
        return pltpu.make_async_remote_copy(
            src_ref=part.at[m, :, 1 - core], dst_ref=sib.at[m],
            send_sem=sib_send.at[m], recv_sem=sib_recv.at[m],
            device_id=sibling, device_id_type=MESH,
        )

    def p_copy(n, stage, d, src, dst, to):
        return pltpu.make_async_remote_copy(
            src_ref=src, dst_ref=dst, send_sem=p_sends.at[n, stage, d], recv_sem=p_recvs.at[n, stage, d],
            device_id=to, device_id_type=MESH,
        )

    def p_first(n, d):
        if n == 0:
            return p_copy(n, 0, d, hp.at[(y + d) % 4, :, 0:40], pr1a.at[d], to_y(d))
        return p_copy(n, 0, d, hp.at[:, (z + d) % 4, 40:80], pr1b.at[d], to_z(d))

    def p_second(n, d):
        if n == 0:
            return p_copy(n, 1, d, ps1a.at[(z + d) % 4], pr2a.at[d], to_z(d))
        return p_copy(n, 1, d, ps1b.at[(y + d) % 4], pr2b.at[d], to_y(d))

    p_sib = p_copy(0, 0, 0, pt_ref.at[:, :, 1 - core], sib_p, sibling)
    p_sib.start()

    bc = bc_ref[...]
    for m in range(SLABS):
        load(m).wait()
        part[m] = dot(li_v[m], bc, TN).reshape(8, 2, 40, 256)
        sib_copy(m).start()
        if m == 1:
            p_sib.wait()
            hp[...] = pt_ref[:, :, core] + sib_p[...]
            for d in (1, 3, 2):
                for n in range(2):
                    p_first(n, d).start()
        if m == 6:
            for n in range(2):
                for d in (1, 2, 3):
                    p_first(n, d).wait()
            ps1a[...] = hp[y, :, 0:40] + pr1a[1] + pr1a[2] + pr1a[3]
            ps1b[...] = hp[:, z, 40:80] + pr1b[1] + pr1b[2] + pr1b[3]
            for d in (1, 3, 2):
                for n in range(2):
                    p_second(n, d).start()
    for m in range(SLABS):
        sib_copy(m).wait()
        h[m // 2, 2 * (m % 2) : 2 * (m % 2) + 2] = (part[m, :, core] + sib[m]).reshape(2, 4, 40, 256)

    def copy(n, stage, d, src, dst, to):
        return pltpu.make_async_remote_copy(
            src_ref=src, dst_ref=dst, send_sem=sends.at[n, stage, d], recv_sem=recvs.at[n, stage, d],
            device_id=to, device_id_type=MESH,
        )

    me = lambda v, d: (v + d) % 4

    def first(n, d):
        lo, hi = ROWS[n]
        size = hi - lo
        rows, cols = pl.ds(lo, size), pl.ds(COLS[n][0], COLS[n][1] - COLS[n][0])
        if n == 0:
            return copy(n, 0, d, h.at[me(x, d), :, :, rows, cols], r1a.at[d], to_x(d))
        if n == 1:
            return copy(n, 0, d, h.at[:, me(y, d), :, rows, cols], r1b.at[d], to_y(d))
        return copy(n, 0, d, h.at[:, :, me(z, d), rows, cols], r1c.at[d], to_z(d))

    def second(n, d):
        if n == 0:
            return copy(n, 1, d, s1a.at[me(y, d)], r2a.at[d], to_y(d))
        if n == 1:
            return copy(n, 1, d, s1b.at[:, me(z, d)], r2b.at[d], to_z(d))
        return copy(n, 1, d, s1c.at[me(x, d)], r2c.at[d], to_x(d))

    def third(n, d):
        if n == 0:
            return copy(n, 2, d, s2a.at[me(z, d)], r3a.at[d], to_z(d))
        if n == 1:
            return copy(n, 2, d, s2b.at[me(x, d)], r3b.at[d], to_x(d))
        return copy(n, 2, d, s2c.at[me(y, d)], r3c.at[d], to_y(d))

    for n in range(2):
        for d in (1, 2, 3):
            p_second(n, d).wait()
    pg_ref[0:40, :] = ps1a[z] + pr2a[1] + pr2a[2] + pr2a[3]
    pg_ref[40:80, :] = ps1b[y] + pr2b[1] + pr2b[2] + pr2b[3]

    each = [(n, d) for d in (1, 3, 2) for n in range(3)]
    for n, d in each:
        first(n, d).start()
    for n in range(3):
        for d in (1, 2, 3):
            first(n, d).wait()
        if n == 0:
            s1a[...] = h[x, :, :, 0:16] + r1a[1] + r1a[2] + r1a[3]
        elif n == 1:
            s1b[...] = h[:, y, :, 16:40, 0:128] + r1b[1] + r1b[2] + r1b[3]
        else:
            s1c[...] = h[:, :, z, 16:40, 128:256] + r1c[1] + r1c[2] + r1c[3]
        for d in (1, 3, 2):
            second(n, d).start()
    for n in range(3):
        for d in (1, 2, 3):
            second(n, d).wait()
        if n == 0:
            s2a[...] = s1a[y] + r2a[1] + r2a[2] + r2a[3]
        elif n == 1:
            s2b[...] = s1b[:, z] + r2b[1] + r2b[2] + r2b[3]
        else:
            s2c[...] = s1c[x] + r2c[1] + r2c[2] + r2c[3]
        for d in (1, 3, 2):
            third(n, d).start()
    for n, (mine, r, at) in enumerate(((s2a, r3a, z), (s2b, r3b, x), (s2c, r3c, y))):
        for d in (1, 2, 3):
            third(n, d).wait()
        out_ref[ROWS[n][0] : ROWS[n][1], COLS[n][0] : COLS[n][1]] = mine[at] + r[1] + r[2] + r[3]


def weight_gradient(li, bc, pterm):
    v = lambda *shape: pltpu.VMEM(shape, F32)
    dma = lambda *n: pltpu.SemaphoreType.DMA(n)
    here = pl.BlockSpec(memory_space=pltpu.VMEM)
    return pl.pallas_call(
        weight_kernel,
        in_specs=[pl.BlockSpec(memory_space=pl.ANY), here, here],
        out_specs=[here, here],
        out_shape=[jax.ShapeDtypeStruct((40, 256), F32), jax.ShapeDtypeStruct((80, 128), F32)],
        scratch_shapes=[
            pltpu.VMEM((SLABS, TOK, SLAB), BF16),
            v(SLABS, 8, 2, 40, 256), v(SLABS, 8, 40, 256), v(4, 4, 4, 40, 256),
            v(4, 4, 80, 128), v(4, 4, 80, 128), v(4, 4, 40, 128), v(4, 4, 40, 128),
            v(4, 40, 128), v(4, 40, 128), v(4, 40, 128), v(4, 40, 128),
            v(4, 4, 4, 16, 256), v(4, 4, 4, 24, 128), v(4, 4, 4, 24, 128),
            v(4, 4, 16, 256), v(4, 4, 24, 128), v(4, 4, 24, 128),
            v(4, 4, 16, 256), v(4, 4, 24, 128), v(4, 4, 24, 128),
            v(4, 16, 256), v(4, 24, 128), v(4, 24, 128),
            v(4, 16, 256), v(4, 24, 128), v(4, 24, 128),
            dma(SLABS), dma(SLABS), dma(SLABS), dma(3, 3, 4), dma(3, 3, 4), dma(2, 2, 4), dma(2, 2, 4),
        ],
        compiler_params=pltpu.CompilerParams(
            collective_id=1, has_side_effects=True, vmem_limit_bytes=VMEM_LIMIT
        ),
    )(li, bc, pterm)


def body(li, x, g, b, c, step, rates, prompt, lens):
    li, x, g, b, c, step, prompt = li[0], x[0], g[0], b[0], c[0], step[0], prompt[0]
    x_grad, bc, pterm = scans(lens, step, rates.reshape(1, HEADS), x, g, b, c, prompt)
    weight_grad, prompt_grad = weight_gradient(li, bc, pterm.reshape(4, 4, 2, 80, 128))
    return x_grad[None], prompt_grad[None], weight_grad


def solution(mesh):
    in_specs = (
        P("group", "seq", None),
        P("group", "seq", None),
        P("group", "seq", None),
        P("group", "seq", None),
        P("group", "seq", None),
        P("group", None, "seq"),
        P(),
        P("group", "seq", None),
        P("group", None),
    )
    out_specs = (P("group", "seq", None), P("group", "seq", None), P(("group", "seq"), None))
    return jax.shard_map(body, mesh=mesh, in_specs=in_specs, out_specs=out_specs, check_vma=False)
```

time: 1170 us -> 117 us (0.10)
  waiting for transfers between devices: 645 us -> 0 us
  other arithmetic: 169 us -> 0 us
  local copies, waits for them, and re-layouts: 136 us -> 3.17 us
  blocking collectives: 132 us -> 0 us
  Pallas kernels: 0 us -> 113 us
  matrix products: 65.1 us -> 0 us
  between operations: 14.7 us -> 0.68 us
    unnamed x6 -> x0, waiting for transfers between devices: 622 us -> none
    unnamed x1 -> x0, blocking collectives: 132 us -> none
    pallas_call x0 -> x2, Pallas kernels: none -> 113 us  [the longest x1 72.6 us: scans(): pl.pallas_call(scan_kernel, in_specs=[pl.BlockSpec(memory_space=pltpu.SME...]
    select_n x65 -> x0, other arithmetic: 105 us -> none  [the longest x64 105 us: step(): return jax.tree.map(lambda a, b: jnp.where(reached, a, b), new, before)]
    dot_general x31 -> x0, matrix products: 65.1 us -> none  [the longest x3 14.3 us: process(): jnp.einsum('thp,shp->hts', grad_block, x_block, preferred_element_type=jn...]
    another operation x18 -> x0, local copies, waits for them, and re-layouts: 36.5 us -> none
    dynamic_update_slice x12 -> x0, other arithmetic: 32.9 us -> none  [body(): lax.map(lambda items: summarize(*items, decay_rates), (x_blocks, grad_blo...]
    unnamed x39 -> x9, local copies, waits for them, and re-layouts: 34.8 us -> 3.17 us
  transfers between devices with their start and end apart: 5 -> 0, of which waited for: 2 -> 0; matrix products, arithmetic and copies ran while one was open for 31% -> 0% of each run, Pallas kernels for 0% -> 0%
where the time goes in v2:
time: 117 us
  Pallas kernels  113 us (97%)
  local copies, waits for them, and re-layouts  3.17 us (3%)
    pallas_call x1, Pallas kernels, scans(): pl.pallas_call(scan_kernel, in_specs=[pl.BlockSpec(memory_space=pltpu.SME...  72.6 us
    pallas_call x1, Pallas kernels, weight_gradient(): pl.pallas_call(weight_kernel, in_specs=[pl.BlockSpec(memory_space=pl.ANY)...  40.8 us
    unnamed x9, local copies, waits for them, and re-layouts  3.17 us

profile of v2, /device:TPU:0, one launch (start us, length us, event | category | flops | bytes accessed | tf_op | source)
XLA Modules:
  0.0 117.3 jit_solution(12510597802314249578)
XLA Ops:
  0.6 72.6 %shard_map.112 = (bf16[768,2560]{1,0:T(8,128)(2,1)}, bf16[768,256]{1,0:T(8,128)(2,1)}, f32[5,8,64,128]{3,2,1,0:T(8,128)}) custom-call(s32[1,4]{1,0:T(1,128)} %lens_ref.1, f32[40,768]{1,0:T(8,128)} %bitcast.18, f32[1,40]{1,0:T(1,128)} %bitcast.21, bf16[768,2560]{1,0:T(8,128)(2,1)} %bitcast.12, bf16[768,2560]{1,0:T(8,128)(2,1)} %bitcast.13, ...), custom_call_target="tpu_custom_call" | custom-call | tf_op jit(solution)/shard_map/pallas_call | solution.py:427
  73.2 0.0 copy-start
  73.3 40.8 %shard_map.113 = (f32[40,256]{1,0:T(8,128)}, f32[80,128]{1,0:T(8,128)}) custom-call(bf16[768,5120]{1,0:T(8,128)(2,1)} %bitcast.11, bf16[768,256]{1,0:T(8,128)(2,1)} %get-tuple-element.9.bc_ref, f32[4,4,2,80,128]{4,3,2,1,0:T(8,128)} %bitcast.15), custom_call_target="tpu_custom_call" | custom-call | tf_op jit(solution)/shard_map/pallas_call | solution.py:617
  114.1 0.0 copy-done
  114.1 0.0 copy-start.2
  114.1 0.0 copy-start.1
  114.1 1.9 %copy.15 = bf16[1,768,2560]{2,1,0:T(8,128)(2,1)} copy(bf16[1,768,2560]{2,1,0:T(8,128)(2,1)S(1)} %bitcast.14) | data formatting | bytes 7864320
  116.1 0.0 copy-done.2
  116.1 0.6 copy.16
  116.7 0.0 copy-done.1
  116.7 0.6 copy.17
Async XLA Ops:
  73.2 40.9 %copy-start = (bf16[768,2560]{1,0:T(8,128)(2,1)S(1)}, bf16[768,2560]{1,0:T(8,128)(2,1)}, u32[]{:S(2)}) copy-start(bf16[768,2560]{1,0:T(8,128)(2,1)} %get-tuple-element.8) | copy-start | bytes 11796484
  114.1 1.9 %copy-start.2 = (f32[80,128]{1,0:T(8,128)S(1)}, f32[80,128]{1,0:T(8,128)}, u32[]{:S(2)}) copy-start(f32[80,128]{1,0:T(8,128)} %get-tuple-element.11) | copy-start | bytes 122884
  114.1 2.6 %copy-start.1 = (f32[40,256]{1,0:T(8,128)S(1)}, f32[40,256]{1,0:T(8,128)}, u32[]{:S(2)}) copy-start(f32[40,256]{1,0:T(8,128)} %get-tuple-element.18) | copy-start | bytes 122884

commit v3 on v2

v3 whole, which is shorter than its diff:
```python
from functools import partial

import jax
import jax.numpy as jnp
from jax import lax
from jax.experimental import pallas as pl
from jax.experimental.pallas import tpu as pltpu
from jax.sharding import PartitionSpec as P

BLOCK = 256
NBLK = 3
TOK = BLOCK * NBLK
HEADS = 40
STATE = 128
WIDTH = 2560
DMODEL = 5120
PHASES = 5
PHEADS = HEADS // PHASES
PLANES = PHEADS * 64
PPAIRS = PHEADS // 2
ROWS = ((0, 16), (16, 40), (16, 40))
COLS = ((0, 256), (0, 128), (128, 256))
SLAB = 640
F32 = jnp.float32
BF16 = jnp.bfloat16
MESH = pl.DeviceIdType.MESH
NN = (((1,), (0,)), ((), ()))
TN = (((0,), (0,)), ((), ()))
NT = (((1,), (1,)), ((), ()))
LOG2E = 1.4426950408889634
VMEM_LIMIT = 62 * 1024 * 1024


def dot(a, b, dims=NN):
    return lax.dot_general(a, b, dims, preferred_element_type=F32)


def iota(shape, dim):
    return lax.broadcasted_iota(jnp.int32, shape, dim)


def flags(lens_ref):
    first = lax.axis_index("seq") * NBLK
    e1 = lens_ref[0, 0]
    e2 = e1 + lens_ref[0, 1]
    e3 = e2 + lens_ref[0, 2]
    e4 = e3 + lens_ref[0, 3]
    not_start, not_last = [], []
    for k in range(NBLK):
        at = first + k
        start = (at == 0) | (at == e1) | (at == e2) | (at == e3)
        last = (at == e1 - 1) | (at == e2 - 1) | (at == e3 - 1) | (at == e4 - 1)
        not_start.append(jnp.where(start, 0.0, 1.0).astype(F32))
        not_last.append(jnp.where(last, 0.0, 1.0).astype(F32))
    return not_start, not_last


def blockrows(k):
    return slice(BLOCK * k, BLOCK * (k + 1))


def gather(table, index):
    return jnp.take_along_axis(table, index, axis=1)


def half_heads(pair, rows):
    return 2 * pair + iota((rows, 128), 1) // 64


def prepare(step_ref, rate_ref, la_v, t1_v, t2_v):
    step = step_ref[...]
    same = iota((HEADS, HEADS), 0) == iota((HEADS, HEADS), 1)
    spread = jnp.broadcast_to(rate_ref[...], (HEADS, HEADS))
    rate = jnp.sum(jnp.where(same, spread, 0.0), axis=1, keepdims=True)
    la = -step * rate
    place = iota((HEADS, TOK), 1) % BLOCK
    shift = 1
    while shift < BLOCK:
        la = la + jnp.where(place >= shift, pltpu.roll(la, shift, 1), 0.0)
        shift *= 2
    la = la * LOG2E
    la_v[...] = la
    ends = [la[:, BLOCK * (k + 1) - 1 : BLOCK * (k + 1)] for k in range(NBLK)]
    end = jnp.concatenate([jnp.broadcast_to(e, (HEADS, BLOCK)) for e in ends], axis=1)
    empty = jnp.zeros((8, TOK), F32)
    t1_v[...] = jnp.concatenate([la, step, jnp.exp2(end - la) * step, empty], axis=0).T
    t2_v[...] = jnp.concatenate([jnp.exp2(la), jnp.zeros((88, TOK), F32)], axis=0).T


def device_coefficients(ns, nl, t1_v):
    dec = [jnp.exp2(t1_v[BLOCK * (k + 1) - 1 : BLOCK * (k + 1), :]) for k in range(NBLK)]
    af = ab = jnp.ones((1, 128), F32)
    pc = jnp.zeros((1, 128), F32)
    for k in range(NBLK):
        af = af * (dec[k] * ns[k])
        pc = dec[k] * (pc * ns[k] + (1.0 - ns[k]))
        ab = ab * (dec[k] * nl[k])
    rows = jnp.concatenate([af, pc, ab, jnp.zeros((5, 128), F32)], axis=0)
    return jnp.where(iota((8, 128), 1) < HEADS, rows, 0.0)


def phase_decays(la_v, j):
    la = la_v[pl.ds(pl.multiple_of(PHEADS * j, PHEADS), PHEADS), :]
    out = []
    for k in range(NBLK):
        at = BLOCK * (k + 1) - 1
        out.append(jnp.broadcast_to(jnp.exp2(la[:, at : at + 1]), (PHEADS, 128))[:, None, :])
    return out


def summarize(j, ns, nl, xg_v, b_ref, c_ref, la_v, t1_v, t2_v, sx_v, sg_v, loc_v, mine):
    ls, lg = [], []
    for k in range(NBLK):
        rows = blockrows(k)
        sx, sg = [], []
        for p in range(PPAIRS):
            lanes = pl.ds(pl.multiple_of(PLANES * j + 128 * p, 128), 128)
            heads = half_heads(PPAIRS * j + p, BLOCK)
            sx.append((xg_v[0, rows, lanes].astype(F32) * gather(t1_v[rows, :], heads + 2 * HEADS)).astype(BF16))
            sg.append((xg_v[1, rows, lanes].astype(F32) * gather(t2_v[rows, :], heads)).astype(BF16))
            sx_v[rows, lanes] = sx[p]
            sg_v[rows, lanes] = sg[p]
        ls.append(dot(jnp.concatenate(sx, axis=1), b_ref[rows, :], TN).reshape(PHEADS, 64, 128))
        lg.append(dot(jnp.concatenate(sg, axis=1), c_ref[rows, :], TN).reshape(PHEADS, 64, 128))
    for n, value in enumerate((ls[0], ls[1], lg[0], lg[1], lg[2])):
        loc_v[j, n] = value
    dec = phase_decays(la_v, j)
    f = ls[0]
    for k in range(1, NBLK):
        f = (dec[k] * ns[k]) * f + ls[k]
    r = lg[2]
    for k in (1, 0):
        r = (dec[k] * nl[k]) * r + lg[k]
    mine[j, :, :, 0:16, :] = f.reshape(16, 2, 16, 128)
    mine[j, :, :, 16:32, :] = r.reshape(16, 2, 16, 128)


def inside_unit(j, k, xg_v, la_v, t1_v, inner_v, pt_v, dx_v):
    r = pl.ds(pl.multiple_of(k * BLOCK, BLOCK), BLOCK)
    table = t1_v[r, :]
    lane = iota((1, 128), 1)
    masks = [jnp.where((lane >= 64) == bool(n), 1.0, 0.0).astype(BF16) for n in range(2)]
    a00, a01, a11 = [], [], []
    for m in range(PPAIRS):
        pair = PPAIRS * j + m
        l = pl.ds(pl.multiple_of(pair * 128, 128), 128)
        g = xg_v[1, r, l]
        xs = (xg_v[0, r, l].astype(F32) * gather(table, half_heads(pair, BLOCK) + HEADS)).astype(BF16)
        gs = [g * m for m in masks]
        low = jnp.concatenate([gs[0][128:], gs[1][128:]], axis=0)
        p0 = dot(jnp.concatenate([xs[:128] * masks[0], xs[:128] * masks[1]], axis=0), g, NT)
        p1 = dot(xs[128:], low, NT)
        w11, d0 = [], []
        for n in range(2):
            row = la_v[pl.ds(2 * pair + n, 1), r]
            col = gather(table, jnp.full((BLOCK, 128), 2 * pair + n, jnp.int32))
            pn = p0[128 * n : 128 * (n + 1)]
            q00 = jnp.exp2(jnp.minimum(row[:, :128] - col[:128], 0.0))
            q01 = jnp.exp2(jnp.minimum(row[:, 128:] - col[:128], 0.0))
            q11 = jnp.exp2(jnp.minimum(row[:, 128:] - col[128:], 0.0))
            a00.append(q00 * pn[:, :128])
            a01.append(q01 * pn[:, 128:])
            a11.append(q11 * p1[:, 128 * n : 128 * (n + 1)])
            w00 = (q00 * inner_v[k, :128, :128]).astype(BF16)
            w01 = (q01 * inner_v[k, :128, 128:]).astype(BF16)
            w11.append((q11 * inner_v[k, 128:, 128:]).astype(BF16))
            d0.append(dot(jnp.concatenate([w00, w01], axis=1), gs[n]))
        d1 = dot(jnp.concatenate(w11, axis=1), low)
        dx_v[r, l] = jnp.concatenate([d0[0] + d0[1], d1], axis=0).astype(BF16)
    pt_v[k, :128, :128] += sum(a00[1:], a00[0])
    pt_v[k, :128, 128:] += sum(a01[1:], a01[0])
    pt_v[k, 128:, 128:] += sum(a11[1:], a11[0])


def gradients(j, ns, nl, b_ref, la_v, t1_v, sx_v, sg_v, loc_v, prompt, el_v, dx_v, acc_v):
    dec = phase_decays(la_v, j)
    el = el_v[j]
    shape = (PHEADS, 64, 128)
    prompt = prompt.reshape(shape)
    state = el[:, :, 0:16].reshape(shape)
    entering = []
    for k in range(NBLK):
        state = state * ns[k] + prompt * (1.0 - ns[k])
        entering.append(state.reshape(PLANES, 128).astype(BF16))
        if k < NBLK - 1:
            state = dec[k] * state + loc_v[j, k]
    state = el[:, :, 16:32].reshape(shape)
    leaving = [None] * NBLK
    total = None
    for k in reversed(range(NBLK)):
        state = state * nl[k]
        leaving[k] = state.reshape(PLANES, 128).astype(BF16)
        state = dec[k] * state + loc_v[j, 2 + k]
        at_start = state * (1.0 - ns[k])
        total = at_start if total is None else total + at_start
    lanes = pl.ds(pl.multiple_of(PLANES * j, PLANES), PLANES)
    for k in range(NBLK):
        rows = blockrows(k)
        outer = dot(b_ref[rows, :], leaving[k], NT)
        table = t1_v[rows, :]
        for p in range(PPAIRS):
            at = pl.ds(pl.multiple_of(PLANES * j + 128 * p, 128), 128)
            heads = half_heads(PPAIRS * j + p, BLOCK)
            near = gather(table, heads + HEADS) * dx_v[rows, at].astype(F32)
            far = gather(table, heads + 2 * HEADS) * outer[:, 128 * p : 128 * (p + 1)]
            dx_v[rows, at] = (near + far).astype(BF16)
        acc_v[rows, :128] += dot(sx_v[rows, lanes], leaving[k])
        acc_v[rows, 128:] += dot(sg_v[rows, lanes], entering[k])
    return total.reshape(32, 16, 128)


TICKS = PHASES + 8


def layer_kernel(
    lens_ref, step_ref, rate_ref, x_hbm, g_hbm, b_ref, c_ref, p_ref, li_hbm,
    xg_hbm, pg_ref, wg_ref,
    xg_v, dx_v, sx_v, sg_v, la_v, t1_v, t2_v, inner_v, pt_v, acc_v, loc_v, bc_v,
    cf_mine, cf_sib, cf_chip, cf_all, mine, sib_in, comb, got, back, ret, sib_out, el_v, prompts,
    pterm, sib_p, hp, pr1a, pr1b, ps1a, ps1b, pr2a, pr2b,
    part, sib, r1a, r1b, r1c, s1a, s1b, s1c, r2a, r2b, r2c, s2a, s2b, s2c, r3a, r3b, r3c,
    x_sem, g_sem, o_sem, c_send, c_recv, f_send, f_recv, l_send, l_recv, p_send, p_recv,
    a_send, a_recv, b_send, b_recv, li_sem, s_send, s_recv, w_send, w_recv, q_send, q_recv,
    w1_send, w1_recv,
):
    group, seq = lax.axis_index("group"), lax.axis_index("seq")
    core = seq % 2
    chip = seq // 2
    y, z = chip // 4, chip % 4
    sibling = (group, chip * 2 + (1 - core))
    is0 = core == 0

    def chip_at(d):
        return ((y + d // 4) % 4) * 4 + (z + d % 4) % 4

    def in_plane(d):
        return (group, chip_at(d) * 2 + core)

    def to_x(d):
        return ((group + d) % 4, seq)

    def to_y(d):
        return in_plane(4 * d)

    def to_z(d):
        return in_plane(d)

    def send(src, dst, s, r, to):
        return pltpu.make_async_remote_copy(
            src_ref=src, dst_ref=dst, send_sem=s, recv_sem=r, device_id=to, device_id_type=MESH
        )

    def lanes(j):
        return pl.ds(pl.multiple_of(PLANES * j, PLANES), PLANES)

    def load_x(j):
        return pltpu.make_async_copy(x_hbm.at[:, lanes(j)], xg_v.at[0, :, lanes(j)], x_sem.at[j])

    def load_g(j):
        return pltpu.make_async_copy(g_hbm.at[:, lanes(j)], xg_v.at[1, :, lanes(j)], g_sem.at[j])

    def load_li(n):
        return pltpu.make_async_copy(li_hbm.at[:, WIDTH * n : WIDTH * (n + 1)], xg_v.at[n], li_sem.at[n])

    def store(j):
        return pltpu.make_async_copy(dx_v.at[:, lanes(j)], xg_hbm.at[:, lanes(j)], o_sem.at[j])

    def each(lo, hi, f):
        def step(i, _):
            f(i)
            return 0

        lax.fori_loop(lo, hi, step, 0)

    def begin(j):
        load_x(j).start()
        load_g(j).start()

    each(0, PHASES, begin)

    barrier = pltpu.get_barrier_semaphore()

    def greet(to):
        pl.semaphore_signal(barrier, inc=1, device_id=to, device_id_type=MESH)

    greet(sibling)
    each(1, 16, lambda d: greet(in_plane(d)))
    each(1, 4, lambda d: greet(to_x(d)))

    prepare(step_ref, rate_ref, la_v, t1_v, t2_v)
    ns, nl = flags(lens_ref)
    cf_mine[...] = device_coefficients(ns, nl, t1_v)

    pl.semaphore_wait(barrier, 19)

    def prompt_copy(d):
        return send(p_ref, prompts.at[chip, core], p_send.at[d], p_recv.at[d], in_plane(d))

    def prompt_pass():
        half = prompts.at[:, core]
        return send(half, half, p_send.at[0], p_recv.at[0], sibling)

    def coefficient_pass():
        return send(cf_mine, cf_sib, c_send.at[0], c_recv.at[0], sibling)

    def coefficient_copy(d):
        return send(cf_chip, cf_all.at[chip], c_send.at[d], c_recv.at[d], in_plane(d))

    def chip_copy(j):
        return send(mine.at[j, :, 1 - core], sib_in.at[j], f_send.at[j], f_recv.at[j], sibling)

    def out_copy(j, d):
        return send(comb.at[j, chip_at(d)], got.at[j, chip], a_send.at[j, d], a_recv.at[j, d], in_plane(d))

    def back_copy(j, d):
        return send(back.at[j, chip_at(d)], ret.at[j, chip], b_send.at[j, d], b_recv.at[j, d], in_plane(d))

    def last_copy(j):
        return send(sib_out.at[j], el_v.at[j, :, core], l_send.at[j], l_recv.at[j], sibling)

    coefficient_pass().start()
    each(1, 16, lambda d: prompt_copy(d).start())
    prompts[chip, core] = p_ref[...]

    def pick(a, b):
        return jnp.where(is0, a, b), jnp.where(is0, b, a)

    def both(j):
        heads = PHEADS * j + iota((16, 128), 0) // 2

        def spread(tile):
            return [
                gather(jnp.broadcast_to(tile[n : n + 1], (16, 128)), heads)[:, None, :] for n in range(3)
            ]

        a, b = pick(mine[j, :, core], sib_in[j])
        t0, t1 = pick(cf_mine[...], cf_sib[...])
        return a, b, spread(t0), spread(t1)

    def combine(j):
        a, b, (_, _, ab0), (af1, _, _) = both(j)
        comb[j, :, 0:16, :] = b[:, 0:16] + af1 * a[:, 0:16]
        comb[j, :, 16:32, :] = a[:, 16:32] + ab0 * b[:, 16:32]

    def piece(j, owner):
        at = 32 * j + owner
        return at // 10, (at // 5) % 2, pl.ds(pl.multiple_of(16 * (at % 5), 16), 16)

    def prompt_rows(j, owner):
        a, b, rows = piece(j, owner)
        return prompts[a, b, rows, :]

    def scan(j):
        own = prompt_rows(j, seq)
        head = jnp.full((128, 128), PHEADS * j + seq // 4, jnp.int32)
        cf = gather(cf_all[...].reshape(128, 128), head)
        e = jnp.zeros((16, 128), F32)
        for q in range(16):
            back[j, q, 0:16, :] = e
            e = cf[8 * q : 8 * q + 1] * e + (cf[8 * q + 1 : 8 * q + 2] * own + got[j, q, 0:16, :])
        lv = jnp.zeros((16, 128), F32)
        for q in reversed(range(16)):
            back[j, q, 16:32, :] = lv
            lv = cf[8 * q + 2 : 8 * q + 3] * lv + got[j, q, 16:32, :]

    def finish(j):
        a, b, (af0, pc0, _), (_, _, ab1) = both(j)
        e0, l1 = ret[j, :, 0:16, :], ret[j, :, 16:32, :]
        prompt = jnp.stack([prompt_rows(j, 2 * q + core) for q in range(16)], axis=0)
        e1 = af0 * e0 + (pc0 * prompt + a[:, 0:16])
        l0 = ab1 * l1 + b[:, 16:32]
        e_mine, e_other = pick(e0, e1)
        l_mine, l_other = pick(l0, l1)
        el_v[j, :, core, 0:16, :] = e_mine
        el_v[j, :, core, 16:32, :] = l_mine
        sib_out[j, :, 0:16, :] = e_other
        sib_out[j, :, 16:32, :] = l_other

    keep = iota((BLOCK, BLOCK), 1) >= iota((BLOCK, BLOCK), 0)

    def tick(t):
        @pl.when(t < PHASES)
        def _():
            load_x(t).wait()
            load_g(t).wait()
            summarize(t, ns, nl, xg_v, b_ref, c_ref, la_v, t1_v, t2_v, sx_v, sg_v, loc_v, mine)
            chip_copy(t).start()

        @pl.when(t == 0)
        def _():
            coefficient_pass().wait()
            t0, t1 = pick(cf_mine[...], cf_sib[...])
            cf_chip[...] = jnp.concatenate(
                [t0[0:1] * t1[0:1], t1[1:2] + t1[0:1] * t0[1:2], t0[2:3] * t1[2:3], t0[3:8]], axis=0
            )
            each(1, 16, lambda d: coefficient_copy(d).start())
            cf_all[chip] = cf_chip[...]

        @pl.when((t >= 1) & (t < PHASES + 1))
        def _():
            j = t - 1
            chip_copy(j).wait()
            combine(j)
            each(1, 16, lambda d: out_copy(j, d).start())
            got[j, chip] = comb[j, chip]

        @pl.when(t == 1)
        def _():
            each(1, 16, lambda d: prompt_copy(d).wait())
            prompt_pass().start()

        @pl.when(t == 3)
        def _():
            prompt_pass().wait()
            each(1, 16, lambda d: coefficient_copy(d).wait())

        @pl.when(t == 4)
        def _():
            for k in range(NBLK):
                rows = blockrows(k)
                inner_v[k] = jnp.where(keep, dot(b_ref[rows, :], c_ref[rows, :], NT), 0.0)
                pt_v[k] = jnp.zeros((BLOCK, BLOCK), F32)
            acc_v[...] = jnp.zeros_like(acc_v)

        @pl.when((t >= 5) & (t < PHASES + 5))
        def _():
            each(0, NBLK, lambda k: inside_unit(t - 5, k, xg_v, la_v, t1_v, inner_v, pt_v, dx_v))

        @pl.when((t >= 4) & (t < PHASES + 4))
        def _():
            j = t - 4
            each(1, 16, lambda d: out_copy(j, d).wait())
            scan(j)
            each(1, 16, lambda d: back_copy(j, d).start())
            ret[j, chip] = back[j, chip]

        @pl.when(t == PHASES + 4)
        def _():
            for n in range(2):
                load_li(n).start()

        @pl.when((t >= 7) & (t < PHASES + 7))
        def _():
            j = t - 7
            each(1, 16, lambda d: back_copy(j, d).wait())
            finish(j)
            last_copy(j).start()

        @pl.when(t >= 8)
        def _():
            j = t - 8
            last_copy(j).wait()
            prompt = jnp.stack([prompt_rows(j, o) for o in range(32)], axis=0)
            total = gradients(j, ns, nl, b_ref, la_v, t1_v, sx_v, sg_v, loc_v, prompt, el_v, dx_v, acc_v)
            store(j).start()
            for o in range(32):
                a, b, rows = piece(j, o)
                pterm[a, b, rows, :] = total[o]

    each(0, TICKS, tick)

    def p_copy(n, stage, d, src, dst, to):
        return send(src, dst, q_send.at[n, stage, d], q_recv.at[n, stage, d], to)

    def p_chip():
        return p_copy(0, 0, 0, pterm.at[:, 1 - core], sib_p, sibling)

    def p_first(n, d):
        if n == 0:
            return p_copy(n, 0, d, hp.at[(y + d) % 4, :, 0:40], pr1a.at[d], to_y(d))
        return p_copy(n, 0, d, hp.at[:, (z + d) % 4, 40:80], pr1b.at[d], to_z(d))

    def p_second(n, d):
        if n == 0:
            return p_copy(n, 1, d, ps1a.at[(z + d) % 4], pr2a.at[d], to_z(d))
        return p_copy(n, 1, d, ps1b.at[(y + d) % 4], pr2b.at[d], to_y(d))

    p_chip().start()
    for k in range(NBLK):
        rows = blockrows(k)
        pt = jnp.where(keep, pt_v[k], 0.0).astype(BF16)
        bc_v[rows, :128] = (acc_v[rows, :128] + dot(pt, c_ref[rows, :])).astype(BF16)
        bc_v[rows, 128:] = (acc_v[rows, 128:] + dot(pt, b_ref[rows, :], TN)).astype(BF16)
    p_chip().wait()
    hp[...] = (pterm[:, core] + sib_p[...]).reshape(4, 4, 80, 128)
    for d in (1, 3, 2):
        for n in range(2):
            p_first(n, d).start()

    def w_copy(n, stage, d, src, dst, to):
        return send(src, dst, w_send.at[n, stage, d], w_recv.at[n, stage, d], to)

    def cut(n):
        return pl.ds(ROWS[n][0], ROWS[n][1] - ROWS[n][0]), pl.ds(COLS[n][0], COLS[n][1] - COLS[n][0])

    def slab_x(s):
        return (group + s) % 4

    def sib_copy(s, n):
        at = slab_x(s)
        return send(
            part.at[at, pl.ds(2 * n, 2), :, 1 - core], sib.at[at, pl.ds(2 * n, 2)],
            s_send.at[s, n], s_recv.at[s, n], sibling,
        )

    def first_x(d):
        return w_copy(0, 0, d, part.at[slab_x(d), :, :, core, *cut(0)], r1a.at[d], to_x(d))

    def first_y(s, d):
        at = slab_x(s)
        return send(
            part.at[at, (y + d) % 4, :, core, *cut(1)], r1b.at[d, at],
            w1_send.at[0, s, d], w1_recv.at[0, s, d], to_y(d),
        )

    def first_z(s, d):
        at = slab_x(s)
        return send(
            part.at[at, :, (z + d) % 4, core, *cut(2)], r1c.at[d, at],
            w1_send.at[1, s, d], w1_recv.at[1, s, d], to_z(d),
        )

    def settle(s):
        at = slab_x(s)
        for n in range(2):
            sib_copy(s, n).wait()
        part[at, :, :, core] = part[at, :, :, core] + sib[at]
        if s > 0:
            first_x(s).start()
        for d in (1, 3, 2):
            first_y(s, d).start()
            first_z(s, d).start()

    for n in range(2):
        load_li(n).wait()
    bc = bc_v[...]
    order = (1, 3, 2, 0)
    for i, s in enumerate(order):
        at = slab_x(s)
        for n in range(2):
            m = at * 2 + n
            cols = pl.ds(pl.multiple_of(SLAB * (m % 4), SLAB), SLAB)
            out = dot(xg_v[m // 4, :, cols], bc, TN)
            part[at, 2 * n : 2 * n + 2] = out.reshape(2, 4, 2, 40, 256)
            sib_copy(s, n).start()
        if i > 0:
            settle(order[i - 1])
    settle(0)

    def second(n, d):
        if n == 0:
            return w_copy(n, 1, d, s1a.at[(y + d) % 4], r2a.at[d], to_y(d))
        if n == 1:
            return w_copy(n, 1, d, s1b.at[:, (z + d) % 4], r2b.at[d], to_z(d))
        return w_copy(n, 1, d, s1c.at[(group + d) % 4], r2c.at[d], to_x(d))

    def third(n, d):
        if n == 0:
            return w_copy(n, 2, d, s2a.at[(z + d) % 4], r3a.at[d], to_z(d))
        if n == 1:
            return w_copy(n, 2, d, s2b.at[(group + d) % 4], r3b.at[d], to_x(d))
        return w_copy(n, 2, d, s2c.at[(y + d) % 4], r3c.at[d], to_y(d))

    for n in range(2):
        for d in (1, 2, 3):
            p_first(n, d).wait()
    ps1a[...] = hp[y, :, 0:40] + pr1a[1] + pr1a[2] + pr1a[3]
    ps1b[...] = hp[:, z, 40:80] + pr1b[1] + pr1b[2] + pr1b[3]
    for d in (1, 3, 2):
        for n in range(2):
            p_second(n, d).start()

    for n in range(3):
        if n == 0:
            for d in (1, 2, 3):
                first_x(d).wait()
            s1a[...] = part[group, :, :, core, 0:16] + r1a[1] + r1a[2] + r1a[3]
        elif n == 1:
            for s in order:
                for d in (1, 2, 3):
                    first_y(s, d).wait()
            s1b[...] = part[:, y, :, core, 16:40, 0:128] + r1b[1] + r1b[2] + r1b[3]
        else:
            for s in order:
                for d in (1, 2, 3):
                    first_z(s, d).wait()
            s1c[...] = part[:, :, z, core, 16:40, 128:256] + r1c[1] + r1c[2] + r1c[3]
        for d in (1, 3, 2):
            second(n, d).start()
    for n in range(3):
        for d in (1, 2, 3):
            second(n, d).wait()
        if n == 0:
            s2a[...] = s1a[y] + r2a[1] + r2a[2] + r2a[3]
        elif n == 1:
            s2b[...] = s1b[:, z] + r2b[1] + r2b[2] + r2b[3]
        else:
            s2c[...] = s1c[group] + r2c[1] + r2c[2] + r2c[3]
        for d in (1, 3, 2):
            third(n, d).start()
    for n in range(2):
        for d in (1, 2, 3):
            p_second(n, d).wait()
    pg_ref[0:40, :] = ps1a[z] + pr2a[1] + pr2a[2] + pr2a[3]
    pg_ref[40:80, :] = ps1b[y] + pr2b[1] + pr2b[2] + pr2b[3]
    for n, (own, r, at) in enumerate(((s2a, r3a, z), (s2b, r3b, group), (s2c, r3c, y))):
        for d in (1, 2, 3):
            third(n, d).wait()
        wg_ref[ROWS[n][0] : ROWS[n][1], COLS[n][0] : COLS[n][1]] = own[at] + r[1] + r[2] + r[3]
    each(0, PHASES, lambda j: store(j).wait())


def layer(lens, step, rates, x, g, b, c, p, li):
    v = pl.BlockSpec(memory_space=pltpu.VMEM)
    a = pl.BlockSpec(memory_space=pl.ANY)
    wide = pltpu.VMEM((TOK, WIDTH), BF16)
    square = pltpu.VMEM((NBLK, BLOCK, BLOCK), F32)
    f = lambda *shape: pltpu.VMEM(shape, F32)
    dma = lambda *n: pltpu.SemaphoreType.DMA(n)
    half = f(PHASES, 16, 32, 128)
    return pl.pallas_call(
        layer_kernel,
        in_specs=[pl.BlockSpec(memory_space=pltpu.SMEM), v, v, a, a, v, v, v, a],
        out_specs=[a, v, v],
        out_shape=[
            jax.ShapeDtypeStruct((TOK, WIDTH), BF16),
            jax.ShapeDtypeStruct((80, 128), F32),
            jax.ShapeDtypeStruct((40, 256), F32),
        ],
        scratch_shapes=[
            pltpu.VMEM((2, TOK, WIDTH), BF16), wide, wide, wide,
            f(HEADS, TOK), f(TOK, 128), f(TOK, 128), square, square, f(TOK, 256),
            f(PHASES, 5, PHEADS, 64, 128), pltpu.VMEM((TOK, 256), BF16),
            f(8, 128), f(8, 128), f(8, 128), f(16, 8, 128),
            f(PHASES, 16, 2, 32, 128), half, half, half, half, half, half,
            f(PHASES, 16, 2, 32, 128), f(16, 2, 80, 128),
            f(16, 2, 80, 128), f(16, 80, 128), f(4, 4, 80, 128), f(4, 4, 40, 128), f(4, 4, 40, 128),
            f(4, 40, 128), f(4, 40, 128), f(4, 40, 128), f(4, 40, 128),
            f(4, 4, 4, 2, 40, 256), f(4, 4, 4, 40, 256),
            f(4, 4, 4, 16, 256), f(4, 4, 4, 24, 128), f(4, 4, 4, 24, 128),
            f(4, 4, 16, 256), f(4, 4, 24, 128), f(4, 4, 24, 128),
            f(4, 4, 16, 256), f(4, 4, 24, 128), f(4, 4, 24, 128),
            f(4, 16, 256), f(4, 24, 128), f(4, 24, 128),
            f(4, 16, 256), f(4, 24, 128), f(4, 24, 128),
            dma(PHASES), dma(PHASES), dma(PHASES), dma(16), dma(16), dma(PHASES), dma(PHASES),
            dma(PHASES), dma(PHASES), dma(16), dma(16), dma(PHASES, 16), dma(PHASES, 16),
            dma(PHASES, 16), dma(PHASES, 16), dma(2), dma(4, 2), dma(4, 2), dma(3, 3, 4), dma(3, 3, 4),
            dma(2, 2, 4), dma(2, 2, 4), dma(2, 4, 4), dma(2, 4, 4),
        ],
        compiler_params=pltpu.CompilerParams(
            collective_id=0, has_side_effects=True, vmem_limit_bytes=VMEM_LIMIT
        ),
    )(lens, step, rates, x, g, b, c, p, li)


def body(li, x, g, b, c, step, rates, prompt, lens):
    li, x, g, b, c, step, prompt = li[0], x[0], g[0], b[0], c[0], step[0], prompt[0]
    x_grad, prompt_grad, weight_grad = layer(
        lens, step, rates.reshape(1, HEADS), x, g, b, c, prompt, li
    )
    return x_grad[None], prompt_grad[None], weight_grad


def solution(mesh):
    in_specs = (
        P("group", "seq", None),
        P("group", "seq", None),
        P("group", "seq", None),
        P("group", "seq", None),
        P("group", "seq", None),
        P("group", None, "seq"),
        P(),
        P("group", "seq", None),
        P("group", None),
    )
    out_specs = (P("group", "seq", None), P("group", "seq", None), P(("group", "seq"), None))
    return jax.shard_map(body, mesh=mesh, in_specs=in_specs, out_specs=out_specs, check_vma=False)
```

time: 117 us -> 97.6 us (0.83)
  Pallas kernels: 113 us -> 90.9 us
  local copies, waits for them, and re-layouts: 3.17 us -> 5.55 us
    pallas_call x2 -> x1, Pallas kernels: 113 us -> 90.9 us  [layer(): pl.pallas_call(layer_kernel, in_specs=[pl.BlockSpec(memory_space=pltpu.SM...]
    unnamed x9 -> x7, local copies, waits for them, and re-layouts: 3.17 us -> 5.55 us
where the time goes in v3:
time: 97.6 us; the launch traced here: 97.1 us
  Pallas kernels  90.9 us (93%)
  local copies, waits for them, and re-layouts  5.55 us (6%)
    pallas_call x1, Pallas kernels, layer(): pl.pallas_call(layer_kernel, in_specs=[pl.BlockSpec(memory_space=pltpu.SM...  90.9 us
    unnamed x7, local copies, waits for them, and re-layouts  5.55 us

profile of v3, /device:TPU:0, one launch (start us, length us, event | category | flops | bytes accessed | tf_op | source)
XLA Modules:
  0.0 97.1 jit_solution(1415798712869573012)
XLA Ops:
  0.6 90.9 %shard_map.112 = (bf16[768,2560]{1,0:T(8,128)(2,1)}, f32[80,128]{1,0:T(8,128)}, f32[40,256]{1,0:T(8,128)}) custom-call(s32[1,4]{1,0:T(1,128)} %lens_ref.1, f32[40,768]{1,0:T(8,128)} %bitcast.16, f32[1,40]{1,0:T(1,128)} %bitcast.19, bf16[768,2560]{1,0:T(8,128)(2,1)} %bitcast.12, bf16[768,2560]{1,0:T(8,128)(2,1)} %bitcast.13, bf16[768,128]{1,0:T(8,128)(2,1)} %bitcast.14, ...), custom_call_target="tpu_custom_call" | custom-call | tf_op jit(solution)/shard_map/pallas_call | solution.py:621
  91.6 0.0 copy-start.1
  91.6 0.0 copy-start
  91.6 4.3 %copy.15 = bf16[1,768,2560]{2,1,0:T(8,128)(2,1)} copy(bf16[1,768,2560]{2,1,0:T(8,128)(2,1)} %bitcast.11) | data formatting | bytes 7864320
  95.9 0.0 copy-done.1
  95.9 0.6 copy.16
  96.5 0.0 copy-done
  96.5 0.6 copy.17
Async XLA Ops:
  91.6 4.3 %copy-start.1 = (f32[80,128]{1,0:T(8,128)S(1)}, f32[80,128]{1,0:T(8,128)}, u32[]{:S(2)}) copy-start(f32[80,128]{1,0:T(8,128)} %get-tuple-element.7) | copy-start | bytes 122884
  91.6 4.9 %copy-start = (f32[40,256]{1,0:T(8,128)S(1)}, f32[40,256]{1,0:T(8,128)}, u32[]{:S(2)}) copy-start(f32[40,256]{1,0:T(8,128)} %get-tuple-element.14) | copy-start | bytes 122884

commit v4 on v3

--- a/solution.py
+++ b/solution.py
@@ -67,7 +67,7 @@
     return 2 * pair + iota((rows, 128), 1) // 64
 
 
-def prepare(step_ref, rate_ref, la_v, t1_v, t2_v):
+def prepare(step_ref, rate_ref, la_v, t1_v, t1b_v, t2b_v):
     step = step_ref[...]
     same = iota((HEADS, HEADS), 0) == iota((HEADS, HEADS), 1)
     spread = jnp.broadcast_to(rate_ref[...], (HEADS, HEADS))
@@ -83,8 +83,10 @@
     ends = [la[:, BLOCK * (k + 1) - 1 : BLOCK * (k + 1)] for k in range(NBLK)]
     end = jnp.concatenate([jnp.broadcast_to(e, (HEADS, BLOCK)) for e in ends], axis=1)
     empty = jnp.zeros((8, TOK), F32)
-    t1_v[...] = jnp.concatenate([la, step, jnp.exp2(end - la) * step, empty], axis=0).T
-    t2_v[...] = jnp.concatenate([jnp.exp2(la), jnp.zeros((88, TOK), F32)], axis=0).T
+    t1 = jnp.concatenate([la, step, jnp.exp2(end - la) * step, empty], axis=0).T
+    t1_v[...] = t1
+    t1b_v[...] = halves(t1)
+    t2b_v[...] = halves(jnp.concatenate([jnp.exp2(la), jnp.zeros((88, TOK), F32)], axis=0).T)
 
 
 def device_coefficients(ns, nl, t1_v):
@@ -99,6 +101,16 @@
     return jnp.where(iota((8, 128), 1) < HEADS, rows, 0.0)
 
 
+def halves(table):
+    high = table.astype(BF16)
+    return jnp.concatenate([high, (table - high.astype(F32)).astype(BF16)], axis=1)
+
+
+def selector(first):
+    row, lane = iota((256, PLANES), 0), iota((256, PLANES), 1)
+    return jnp.where(row % 128 == first + lane // 64, 1.0, 0.0).astype(BF16)
+
+
 def phase_decays(la_v, j):
     la = la_v[pl.ds(pl.multiple_of(PHEADS * j, PHEADS), PHEADS), :]
     out = []
@@ -108,16 +120,19 @@
     return out
 
 
-def summarize(j, ns, nl, xg_v, b_ref, c_ref, la_v, t1_v, t2_v, sx_v, sg_v, loc_v, mine):
+def summarize(j, ns, nl, xg_v, b_ref, c_ref, la_v, t1b_v, t2b_v, sx_v, sg_v, loc_v, mine):
     ls, lg = [], []
     for k in range(NBLK):
         rows = blockrows(k)
         sx, sg = [], []
+        ex = dot(t1b_v[rows, :], selector(2 * HEADS + PHEADS * j))
+        eg = dot(t2b_v[rows, :], selector(PHEADS * j))
         for p in range(PPAIRS):
             lanes = pl.ds(pl.multiple_of(PLANES * j + 128 * p, 128), 128)
             heads = half_heads(PPAIRS * j + p, BLOCK)
-            sx.append((xg_v[0, rows, lanes].astype(F32) * gather(t1_v[rows, :], heads + 2 * HEADS)).astype(BF16))
-            sg.append((xg_v[1, rows, lanes].astype(F32) * gather(t2_v[rows, :], heads)).astype(BF16))
+            wx, wg = ex[:, 128 * p : 128 * (p + 1)], eg[:, 128 * p : 128 * (p + 1)]
+            sx.append((xg_v[0, rows, lanes].astype(F32) * wx).astype(BF16))
+            sg.append((xg_v[1, rows, lanes].astype(F32) * wg).astype(BF16))
             sx_v[rows, lanes] = sx[p]
             sg_v[rows, lanes] = sg[p]
         ls.append(dot(jnp.concatenate(sx, axis=1), b_ref[rows, :], TN).reshape(PHEADS, 64, 128))
@@ -172,7 +187,7 @@
     pt_v[k, 128:, 128:] += sum(a11[1:], a11[0])
 
 
-def gradients(j, ns, nl, b_ref, la_v, t1_v, sx_v, sg_v, loc_v, prompt, el_v, dx_v, acc_v):
+def gradients(j, ns, nl, b_ref, la_v, t1b_v, sx_v, sg_v, loc_v, prompt, el_v, dx_v, acc_v):
     dec = phase_decays(la_v, j)
     el = el_v[j]
     shape = (PHEADS, 64, 128)
@@ -197,12 +212,14 @@
     for k in range(NBLK):
         rows = blockrows(k)
         outer = dot(b_ref[rows, :], leaving[k], NT)
-        table = t1_v[rows, :]
+        near_w = dot(t1b_v[rows, :], selector(HEADS + PHEADS * j))
+        far_w = dot(t1b_v[rows, :], selector(2 * HEADS + PHEADS * j))
         for p in range(PPAIRS):
+            cut = slice(128 * p, 128 * (p + 1))
             at = pl.ds(pl.multiple_of(PLANES * j + 128 * p, 128), 128)
             heads = half_heads(PPAIRS * j + p, BLOCK)
-            near = gather(table, heads + HEADS) * dx_v[rows, at].astype(F32)
-            far = gather(table, heads + 2 * HEADS) * outer[:, 128 * p : 128 * (p + 1)]
+            near = near_w[:, cut] * dx_v[rows, at].astype(F32)
+            far = far_w[:, cut] * outer[:, cut]
             dx_v[rows, at] = (near + far).astype(BF16)
         acc_v[rows, :128] += dot(sx_v[rows, lanes], leaving[k])
         acc_v[rows, 128:] += dot(sg_v[rows, lanes], entering[k])
@@ -215,13 +232,12 @@
 def layer_kernel(
     lens_ref, step_ref, rate_ref, x_hbm, g_hbm, b_ref, c_ref, p_ref, li_hbm,
     xg_hbm, pg_ref, wg_ref,
-    xg_v, dx_v, sx_v, sg_v, la_v, t1_v, t2_v, inner_v, pt_v, acc_v, loc_v, bc_v,
+    xg_v, dx_v, sx_v, sg_v, la_v, t1_v, t1b_v, t2b_v, inner_v, pt_v, acc_v, loc_v, bc_v,
     cf_mine, cf_sib, cf_chip, cf_all, mine, sib_in, comb, got, back, ret, sib_out, el_v, prompts,
-    pterm, sib_p, hp, pr1a, pr1b, ps1a, ps1b, pr2a, pr2b,
+    pterm, sib_p, pr1a, pr1b, ps1a, ps1b, pr2a, pr2b,
     part, sib, r1a, r1b, r1c, s1a, s1b, s1c, r2a, r2b, r2c, s2a, s2b, s2c, r3a, r3b, r3c,
     x_sem, g_sem, o_sem, c_send, c_recv, f_send, f_recv, l_send, l_recv, p_send, p_recv,
     a_send, a_recv, b_send, b_recv, li_sem, s_send, s_recv, w_send, w_recv, q_send, q_recv,
-    w1_send, w1_recv,
 ):
     group, seq = lax.axis_index("group"), lax.axis_index("seq")
     core = seq % 2
@@ -263,7 +279,7 @@
         return pltpu.make_async_copy(li_hbm.at[:, WIDTH * n : WIDTH * (n + 1)], xg_v.at[n], li_sem.at[n])
 
     def store(j):
-        return pltpu.make_async_copy(dx_v.at[:, lanes(j)], xg_hbm.at[:, lanes(j)], o_sem.at[j])
+        return pltpu.make_async_copy(dx_v.at[:, lanes(j)], xg_hbm.at[:, lanes(j)], o_sem.at[0])
 
     def each(lo, hi, f):
         def step(i, _):
@@ -287,14 +303,24 @@
     each(1, 16, lambda d: greet(in_plane(d)))
     each(1, 4, lambda d: greet(to_x(d)))
 
-    prepare(step_ref, rate_ref, la_v, t1_v, t2_v)
+    prepare(step_ref, rate_ref, la_v, t1_v, t1b_v, t2b_v)
     ns, nl = flags(lens_ref)
     cf_mine[...] = device_coefficients(ns, nl, t1_v)
 
+    def start_phase(t):
+        load_x(t).wait()
+        load_g(t).wait()
+        summarize(t, ns, nl, xg_v, b_ref, c_ref, la_v, t1b_v, t2b_v, sx_v, sg_v, loc_v, mine)
+
+    start_phase(0)
     pl.semaphore_wait(barrier, 19)
 
     def prompt_copy(d):
-        return send(p_ref, prompts.at[chip, core], p_send.at[d], p_recv.at[d], in_plane(d))
+        return send(p_ref, prompts.at[chip, core], p_send.at[1], p_recv.at[1], in_plane(d))
+
+    def prompt_all():
+        some = prompts.at[pl.ds(0, 15), 0]
+        return send(some, some, p_send.at[1], p_recv.at[1], sibling)
 
     def prompt_pass():
         half = prompts.at[:, core]
@@ -304,21 +330,34 @@
         return send(cf_mine, cf_sib, c_send.at[0], c_recv.at[0], sibling)
 
     def coefficient_copy(d):
-        return send(cf_chip, cf_all.at[chip], c_send.at[d], c_recv.at[d], in_plane(d))
+        return send(cf_chip, cf_all.at[chip], c_send.at[1], c_recv.at[1], in_plane(d))
+
+    def coefficient_all():
+        some = cf_all.at[pl.ds(0, 15)]
+        return send(some, some, c_send.at[1], c_recv.at[1], sibling)
 
     def chip_copy(j):
         return send(mine.at[j, :, 1 - core], sib_in.at[j], f_send.at[j], f_recv.at[j], sibling)
 
     def out_copy(j, d):
-        return send(comb.at[j, chip_at(d)], got.at[j, chip], a_send.at[j, d], a_recv.at[j, d], in_plane(d))
+        return send(comb.at[j, chip_at(d)], got.at[j, chip], a_send.at[j], a_recv.at[j], in_plane(d))
+
+    def out_all(j):
+        some = pl.ds(0, 15)
+        return send(comb.at[j, some], got.at[j, some], a_send.at[j], a_recv.at[j], sibling)
 
     def back_copy(j, d):
-        return send(back.at[j, chip_at(d)], ret.at[j, chip], b_send.at[j, d], b_recv.at[j, d], in_plane(d))
+        return send(back.at[j, chip_at(d)], ret.at[j, chip], b_send.at[j], b_recv.at[j], in_plane(d))
+
+    def back_all(j):
+        some = pl.ds(0, 15)
+        return send(back.at[j, some], ret.at[j, some], b_send.at[j], b_recv.at[j], sibling)
 
     def last_copy(j):
         return send(sib_out.at[j], el_v.at[j, :, core], l_send.at[j], l_recv.at[j], sibling)
 
     coefficient_pass().start()
+    chip_copy(0).start()
     each(1, 16, lambda d: prompt_copy(d).start())
     prompts[chip, core] = p_ref[...]
 
@@ -381,12 +420,10 @@
     def tick(t):
         @pl.when(t < PHASES)
         def _():
-            load_x(t).wait()
-            load_g(t).wait()
-            summarize(t, ns, nl, xg_v, b_ref, c_ref, la_v, t1_v, t2_v, sx_v, sg_v, loc_v, mine)
+            start_phase(t)
             chip_copy(t).start()
 
-        @pl.when(t == 0)
+        @pl.when(t == 1)
         def _():
             coefficient_pass().wait()
             t0, t1 = pick(cf_mine[...], cf_sib[...])
@@ -396,7 +433,7 @@
             each(1, 16, lambda d: coefficient_copy(d).start())
             cf_all[chip] = cf_chip[...]
 
-        @pl.when((t >= 1) & (t < PHASES + 1))
+        @pl.when(t < PHASES + 1)
         def _():
             j = t - 1
             chip_copy(j).wait()
@@ -404,15 +441,15 @@
             each(1, 16, lambda d: out_copy(j, d).start())
             got[j, chip] = comb[j, chip]
 
-        @pl.when(t == 1)
-        def _():
-            each(1, 16, lambda d: prompt_copy(d).wait())
+        @pl.when(t == 2)
+        def _():
+            prompt_all().wait()
             prompt_pass().start()
 
         @pl.when(t == 3)
         def _():
             prompt_pass().wait()
-            each(1, 16, lambda d: coefficient_copy(d).wait())
+            coefficient_all().wait()
 
         @pl.when(t == 4)
         def _():
@@ -429,7 +466,7 @@
         @pl.when((t >= 4) & (t < PHASES + 4))
         def _():
             j = t - 4
-            each(1, 16, lambda d: out_copy(j, d).wait())
+            out_all(j).wait()
             scan(j)
             each(1, 16, lambda d: back_copy(j, d).start())
             ret[j, chip] = back[j, chip]
@@ -442,7 +479,7 @@
         @pl.when((t >= 7) & (t < PHASES + 7))
         def _():
             j = t - 7
-            each(1, 16, lambda d: back_copy(j, d).wait())
+            back_all(j).wait()
             finish(j)
             last_copy(j).start()
 
@@ -451,24 +488,24 @@
             j = t - 8
             last_copy(j).wait()
             prompt = jnp.stack([prompt_rows(j, o) for o in range(32)], axis=0)
-            total = gradients(j, ns, nl, b_ref, la_v, t1_v, sx_v, sg_v, loc_v, prompt, el_v, dx_v, acc_v)
+            total = gradients(j, ns, nl, b_ref, la_v, t1b_v, sx_v, sg_v, loc_v, prompt, el_v, dx_v, acc_v)
             store(j).start()
             for o in range(32):
                 a, b, rows = piece(j, o)
-                pterm[a, b, rows, :] = total[o]
-
-    each(0, TICKS, tick)
+                pterm[a // 4, a % 4, b, rows, :] = total[o]
+
+    each(1, TICKS, tick)
 
     def p_copy(n, stage, d, src, dst, to):
-        return send(src, dst, q_send.at[n, stage, d], q_recv.at[n, stage, d], to)
+        return send(src, dst, q_send.at[n, stage], q_recv.at[n, stage], to)
 
     def p_chip():
-        return p_copy(0, 0, 0, pterm.at[:, 1 - core], sib_p, sibling)
+        return p_copy(2, 0, 0, pterm.at[:, :, 1 - core], sib_p, sibling)
 
     def p_first(n, d):
         if n == 0:
-            return p_copy(n, 0, d, hp.at[(y + d) % 4, :, 0:40], pr1a.at[d], to_y(d))
-        return p_copy(n, 0, d, hp.at[:, (z + d) % 4, 40:80], pr1b.at[d], to_z(d))
+            return p_copy(n, 0, d, pterm.at[(y + d) % 4, :, core, 0:40], pr1a.at[d], to_y(d))
+        return p_copy(n, 0, d, pterm.at[:, (z + d) % 4, core, 40:80], pr1b.at[d], to_z(d))
 
     def p_second(n, d):
         if n == 0:
@@ -481,14 +518,8 @@
         pt = jnp.where(keep, pt_v[k], 0.0).astype(BF16)
         bc_v[rows, :128] = (acc_v[rows, :128] + dot(pt, c_ref[rows, :])).astype(BF16)
         bc_v[rows, 128:] = (acc_v[rows, 128:] + dot(pt, b_ref[rows, :], TN)).astype(BF16)
-    p_chip().wait()
-    hp[...] = (pterm[:, core] + sib_p[...]).reshape(4, 4, 80, 128)
-    for d in (1, 3, 2):
-        for n in range(2):
-            p_first(n, d).start()
-
     def w_copy(n, stage, d, src, dst, to):
-        return send(src, dst, w_send.at[n, stage, d], w_recv.at[n, stage, d], to)
+        return send(src, dst, w_send.at[n, stage], w_recv.at[n, stage], to)
 
     def cut(n):
         return pl.ds(ROWS[n][0], ROWS[n][1] - ROWS[n][0]), pl.ds(COLS[n][0], COLS[n][1] - COLS[n][0])
@@ -500,30 +531,33 @@
         at = slab_x(s)
         return send(
             part.at[at, pl.ds(2 * n, 2), :, 1 - core], sib.at[at, pl.ds(2 * n, 2)],
-            s_send.at[s, n], s_recv.at[s, n], sibling,
+            s_send.at[s], s_recv.at[s], sibling,
         )
 
+    def sib_all(s):
+        at = slab_x(s)
+        return send(part.at[at, :, :, 1 - core], sib.at[at], s_send.at[s], s_recv.at[s], sibling)
+
     def first_x(d):
-        return w_copy(0, 0, d, part.at[slab_x(d), :, :, core, *cut(0)], r1a.at[d], to_x(d))
+        return w_copy(0, 0, d, part.at[slab_x(d), :, :, core, *cut(0)], r1a.at[d - 1], to_x(d))
 
     def first_y(s, d):
         at = slab_x(s)
         return send(
-            part.at[at, (y + d) % 4, :, core, *cut(1)], r1b.at[d, at],
-            w1_send.at[0, s, d], w1_recv.at[0, s, d], to_y(d),
+            part.at[at, (y + d) % 4, :, core, *cut(1)], r1b.at[d - 1, at],
+            w_send.at[1, 0], w_recv.at[1, 0], to_y(d),
         )
 
     def first_z(s, d):
         at = slab_x(s)
         return send(
-            part.at[at, :, (z + d) % 4, core, *cut(2)], r1c.at[d, at],
-            w1_send.at[1, s, d], w1_recv.at[1, s, d], to_z(d),
+            part.at[at, :, (z + d) % 4, core, *cut(2)], r1c.at[d - 1, at],
+            w_send.at[2, 0], w_recv.at[2, 0], to_z(d),
         )
 
     def settle(s):
         at = slab_x(s)
-        for n in range(2):
-            sib_copy(s, n).wait()
+        sib_all(s).wait()
         part[at, :, :, core] = part[at, :, :, core] + sib[at]
         if s > 0:
             first_x(s).start()
@@ -543,7 +577,13 @@
             out = dot(xg_v[m // 4, :, cols], bc, TN)
             part[at, 2 * n : 2 * n + 2] = out.reshape(2, 4, 2, 40, 256)
             sib_copy(s, n).start()
-        if i > 0:
+        if i == 0:
+            p_chip().wait()
+            pterm[:, :, core] = pterm[:, :, core] + sib_p[...]
+            for d in (1, 3, 2):
+                for q in range(2):
+                    p_first(q, d).start()
+        else:
             settle(order[i - 1])
     settle(0)
 
@@ -561,35 +601,30 @@
             return w_copy(n, 2, d, s2b.at[(group + d) % 4], r3b.at[d], to_x(d))
         return w_copy(n, 2, d, s2c.at[(y + d) % 4], r3c.at[d], to_y(d))
 
-    for n in range(2):
-        for d in (1, 2, 3):
-            p_first(n, d).wait()
-    ps1a[...] = hp[y, :, 0:40] + pr1a[1] + pr1a[2] + pr1a[3]
-    ps1b[...] = hp[:, z, 40:80] + pr1b[1] + pr1b[2] + pr1b[3]
+    three = pl.ds(1, 3)
+    peers = pl.ds(0, 3)
+    p_copy(0, 0, 1, pterm.at[peers, :, 0, 0:40], pr1a.at[three], sibling).wait()
+    p_copy(1, 0, 1, pterm.at[peers, :, 0, 40:80], pr1b.at[three], sibling).wait()
+    ps1a[...] = pterm[y, :, core, 0:40] + pr1a[1] + pr1a[2] + pr1a[3]
+    ps1b[...] = pterm[:, z, core, 40:80] + pr1b[1] + pr1b[2] + pr1b[3]
     for d in (1, 3, 2):
         for n in range(2):
             p_second(n, d).start()
 
     for n in range(3):
         if n == 0:
-            for d in (1, 2, 3):
-                first_x(d).wait()
-            s1a[...] = part[group, :, :, core, 0:16] + r1a[1] + r1a[2] + r1a[3]
+            w_copy(0, 0, 1, r1a, r1a, sibling).wait()
+            s1a[...] = part[group, :, :, core, 0:16] + r1a[0] + r1a[1] + r1a[2]
         elif n == 1:
-            for s in order:
-                for d in (1, 2, 3):
-                    first_y(s, d).wait()
-            s1b[...] = part[:, y, :, core, 16:40, 0:128] + r1b[1] + r1b[2] + r1b[3]
+            w_copy(1, 0, 1, r1b, r1b, sibling).wait()
+            s1b[...] = part[:, y, :, core, 16:40, 0:128] + r1b[0] + r1b[1] + r1b[2]
         else:
-            for s in order:
-                for d in (1, 2, 3):
-                    first_z(s, d).wait()
-            s1c[...] = part[:, :, z, core, 16:40, 128:256] + r1c[1] + r1c[2] + r1c[3]
+            w_copy(2, 0, 1, r1c, r1c, sibling).wait()
+            s1c[...] = part[:, :, z, core, 16:40, 128:256] + r1c[0] + r1c[1] + r1c[2]
         for d in (1, 3, 2):
             second(n, d).start()
-    for n in range(3):
-        for d in (1, 2, 3):
-            second(n, d).wait()
+    for n, r in enumerate((r2a, r2b, r2c)):
+        w_copy(n, 1, 1, r.at[three], r.at[three], sibling).wait()
         if n == 0:
             s2a[...] = s1a[y] + r2a[1] + r2a[2] + r2a[3]
         elif n == 1:
@@ -598,16 +633,14 @@
             s2c[...] = s1c[group] + r2c[1] + r2c[2] + r2c[3]
         for d in (1, 3, 2):
             third(n, d).start()
-    for n in range(2):
-        for d in (1, 2, 3):
-            p_second(n, d).wait()
+    p_copy(0, 1, 1, pr2a.at[three], pr2a.at[three], sibling).wait()
+    p_copy(1, 1, 1, pr2b.at[three], pr2b.at[three], sibling).wait()
     pg_ref[0:40, :] = ps1a[z] + pr2a[1] + pr2a[2] + pr2a[3]
     pg_ref[40:80, :] = ps1b[y] + pr2b[1] + pr2b[2] + pr2b[3]
     for n, (own, r, at) in enumerate(((s2a, r3a, z), (s2b, r3b, group), (s2c, r3c, y))):
-        for d in (1, 2, 3):
-            third(n, d).wait()
+        w_copy(n, 2, 1, r.at[three], r.at[three], sibling).wait()
         wg_ref[ROWS[n][0] : ROWS[n][1], COLS[n][0] : COLS[n][1]] = own[at] + r[1] + r[2] + r[3]
-    each(0, PHASES, lambda j: store(j).wait())
+    pltpu.make_async_copy(dx_v, xg_hbm, o_sem.at[0]).wait()
 
 
 def layer(lens, step, rates, x, g, b, c, p, li):
@@ -629,23 +662,22 @@
         ],
         scratch_shapes=[
             pltpu.VMEM((2, TOK, WIDTH), BF16), wide, wide, wide,
-            f(HEADS, TOK), f(TOK, 128), f(TOK, 128), square, square, f(TOK, 256),
+            f(HEADS, TOK), f(TOK, 128), pltpu.VMEM((TOK, 256), BF16), pltpu.VMEM((TOK, 256), BF16), square, square, f(TOK, 256),
             f(PHASES, 5, PHEADS, 64, 128), pltpu.VMEM((TOK, 256), BF16),
             f(8, 128), f(8, 128), f(8, 128), f(16, 8, 128),
             f(PHASES, 16, 2, 32, 128), half, half, half, half, half, half,
             f(PHASES, 16, 2, 32, 128), f(16, 2, 80, 128),
-            f(16, 2, 80, 128), f(16, 80, 128), f(4, 4, 80, 128), f(4, 4, 40, 128), f(4, 4, 40, 128),
+            f(4, 4, 2, 80, 128), f(4, 4, 80, 128), f(4, 4, 40, 128), f(4, 4, 40, 128),
             f(4, 40, 128), f(4, 40, 128), f(4, 40, 128), f(4, 40, 128),
             f(4, 4, 4, 2, 40, 256), f(4, 4, 4, 40, 256),
-            f(4, 4, 4, 16, 256), f(4, 4, 4, 24, 128), f(4, 4, 4, 24, 128),
+            f(3, 4, 4, 16, 256), f(3, 4, 4, 24, 128), f(3, 4, 4, 24, 128),
             f(4, 4, 16, 256), f(4, 4, 24, 128), f(4, 4, 24, 128),
             f(4, 4, 16, 256), f(4, 4, 24, 128), f(4, 4, 24, 128),
             f(4, 16, 256), f(4, 24, 128), f(4, 24, 128),
             f(4, 16, 256), f(4, 24, 128), f(4, 24, 128),
-            dma(PHASES), dma(PHASES), dma(PHASES), dma(16), dma(16), dma(PHASES), dma(PHASES),
-            dma(PHASES), dma(PHASES), dma(16), dma(16), dma(PHASES, 16), dma(PHASES, 16),
-            dma(PHASES, 16), dma(PHASES, 16), dma(2), dma(4, 2), dma(4, 2), dma(3, 3, 4), dma(3, 3, 4),
-            dma(2, 2, 4), dma(2, 2, 4), dma(2, 4, 4), dma(2, 4, 4),
+            dma(PHASES), dma(PHASES), dma(1), dma(2), dma(2), dma(PHASES), dma(PHASES),
+            dma(PHASES), dma(PHASES), dma(2), dma(2), dma(PHASES), dma(PHASES),
+            dma(PHASES), dma(PHASES), dma(2), dma(4), dma(4), dma(3, 3), dma(3, 3), dma(3, 2), dma(3, 2),
         ],
         compiler_params=pltpu.CompilerParams(
             collective_id=0, has_side_effects=True, vmem_limit_bytes=VMEM_LIMIT
@@ -653,11 +685,51 @@
     )(lens, step, rates, x, g, b, c, p, li)
 
 
+def deliver_kernel(x_hbm, p_ref, w_ref, xo_hbm, po_ref, wo_ref, hold, sems):
+    def into(n):
+        rows = pl.ds(n * PIECE, PIECE)
+        return pltpu.make_async_copy(x_hbm.at[rows], hold.at[n], sems.at[0, n])
+
+    def out(n):
+        rows = pl.ds(n * PIECE, PIECE)
+        return pltpu.make_async_copy(hold.at[n], xo_hbm.at[rows], sems.at[1, n])
+
+    count = TOK // PIECE
+    for n in range(count):
+        into(n).start()
+    po_ref[...] = p_ref[...]
+    wo_ref[...] = w_ref[...]
+    for n in range(count):
+        into(n).wait()
+        out(n).start()
+    for n in range(count):
+        out(n).wait()
+
+
+PIECE = 96
+
+
+def deliver(x, p, w):
+    v = pl.BlockSpec(memory_space=pltpu.VMEM)
+    a = pl.BlockSpec(memory_space=pl.ANY)
+    return pl.pallas_call(
+        deliver_kernel,
+        in_specs=[a, v, v],
+        out_specs=[a, v, v],
+        out_shape=[jax.ShapeDtypeStruct(t.shape, t.dtype) for t in (x, p, w)],
+        scratch_shapes=[
+            pltpu.VMEM((TOK // PIECE, PIECE, WIDTH), BF16), pltpu.SemaphoreType.DMA((2, TOK // PIECE))
+        ],
+        compiler_params=pltpu.CompilerParams(vmem_limit_bytes=16 * 1024 * 1024),
+    )(x, p, w)
+
+
 def body(li, x, g, b, c, step, rates, prompt, lens):
     li, x, g, b, c, step, prompt = li[0], x[0], g[0], b[0], c[0], step[0], prompt[0]
     x_grad, prompt_grad, weight_grad = layer(
         lens, step, rates.reshape(1, HEADS), x, g, b, c, prompt, li
     )
+    x_grad, prompt_grad, weight_grad = deliver(x_grad, prompt_grad, weight_grad)
     return x_grad[None], prompt_grad[None], weight_grad
 
 

time: 97.6 us -> 93.2 us (0.955)
  Pallas kernels: 90.9 us -> 88.1 us
  local copies, waits for them, and re-layouts: 5.55 us -> 3.66 us
    pallas_call x1, Pallas kernels: 90.9 us -> 82.9 us  [layer(): pl.pallas_call(layer_kernel, in_specs=[pl.BlockSpec(memory_space=pltpu.SM...]
    pallas_call x0 -> x1, Pallas kernels: none -> 5.18 us  [deliver(): pl.pallas_call(deliver_kernel, in_specs=[a, v, v], out_specs=[a, v, v], o...]
    unnamed x7 -> x6, local copies, waits for them, and re-layouts: 5.55 us -> 3.66 us
where the time goes in v4:
time: 93.2 us; the launch traced here: 92.4 us
  Pallas kernels  88.1 us (95%)
  local copies, waits for them, and re-layouts  3.66 us (4%)
    pallas_call x1, Pallas kernels, layer(): pl.pallas_call(layer_kernel, in_specs=[pl.BlockSpec(memory_space=pltpu.SM...  82.9 us
    pallas_call x1, Pallas kernels, deliver(): pl.pallas_call(deliver_kernel, in_specs=[a, v, v], out_specs=[a, v, v], o...  5.18 us
    unnamed x6, local copies, waits for them, and re-layouts  3.66 us

profile of v4, /device:TPU:0, one launch (start us, length us, event | category | flops | bytes accessed | tf_op | source)
XLA Modules:
  0.0 92.4 jit_solution(1283769495487874480)
XLA Ops:
  0.6 82.9 %shard_map.112 = (bf16[768,2560]{1,0:T(8,128)(2,1)}, f32[80,128]{1,0:T(8,128)}, f32[40,256]{1,0:T(8,128)}) custom-call(s32[1,4]{1,0:T(1,128)} %lens_ref.1, f32[40,768]{1,0:T(8,128)} %bitcast.15, f32[1,40]{1,0:T(1,128)} %bitcast.17, bf16[768,2560]{1,0:T(8,128)(2,1)} %bitcast.11, bf16[768,2560]{1,0:T(8,128)(2,1)} %bitcast.12, bf16[768,128]{1,0:T(8,128)(2,1)} %bitcast.13, ...), custom_call_target="tpu_custom_call" | custom-call | tf_op jit(solution)/shard_map/pallas_call | solution.py:654
  83.6 0.0 copy-start
  83.6 2.1 %copy-done = bf16[768,2560]{1,0:T(8,128)(2,1)S(1)} copy-done((bf16[768,2560]{1,0:T(8,128)(2,1)S(1)}, bf16[768,2560]{1,0:T(8,128)(2,1)}, u32[]{:S(2)}) %copy-start) | copy-done | bytes 3932184
  85.7 0.0 copy-start.1
  85.7 0.8 copy-done.1
  86.4 0.0 copy-start.2
  86.4 0.8 copy-done.2
  87.2 5.2 %shard_map.113 = (bf16[768,2560]{1,0:T(8,128)(2,1)}, f32[80,128]{1,0:T(8,128)}, f32[40,256]{1,0:T(8,128)}) custom-call(bf16[768,2560]{1,0:T(8,128)(2,1)S(1)} %copy-done, f32[80,128]{1,0:T(8,128)S(1)} %copy-done.1, f32[40,256]{1,0:T(8,128)S(1)} %copy-done.2), custom_call_target="tpu_custom_call" | custom-call | tf_op jit(solution)/shard_map/pallas_call | solution.py:715
Async XLA Ops:
  83.6 2.1 %copy-start = (bf16[768,2560]{1,0:T(8,128)(2,1)S(1)}, bf16[768,2560]{1,0:T(8,128)(2,1)}, u32[]{:S(2)}) copy-start(bf16[768,2560]{1,0:T(8,128)(2,1)} %get-tuple-element.9.x_hbm) | copy-start | bytes 11796484
  85.7 0.8 copy-start.1
  86.4 0.8 copy-start.2

commit v5 on v4

--- a/solution.py
+++ b/solution.py
@@ -720,7 +720,7 @@
         scratch_shapes=[
             pltpu.VMEM((TOK // PIECE, PIECE, WIDTH), BF16), pltpu.SemaphoreType.DMA((2, TOK // PIECE))
         ],
-        compiler_params=pltpu.CompilerParams(vmem_limit_bytes=16 * 1024 * 1024),
+        compiler_params=pltpu.CompilerParams(vmem_limit_bytes=VMEM_LIMIT),
     )(x, p, w)
 
 

time: 93.2 us -> 88.9 us (0.954)
  local copies, waits for them, and re-layouts: 3.66 us -> 0 us
    unnamed x6 -> x0, local copies, waits for them, and re-layouts: 3.66 us -> none
where the time goes in v5:
time: 88.9 us; the launch traced here: 88.3 us
  Pallas kernels  87.6 us (99%)
    pallas_call x1, Pallas kernels, layer(): pl.pallas_call(layer_kernel, in_specs=[pl.BlockSpec(memory_space=pltpu.SM...  82.9 us
    pallas_call x1, Pallas kernels, deliver(): pl.pallas_call(deliver_kernel, in_specs=[a, v, v], out_specs=[a, v, v], o...  4.74 us

profile of v5, /device:TPU:0, one launch (start us, length us, event | category | flops | bytes accessed | tf_op | source)
XLA Modules:
  0.0 88.3 jit_solution(6413047827011034986)
XLA Ops:
  0.6 82.9 %shard_map.112 = (bf16[768,2560]{1,0:T(8,128)(2,1)}, f32[80,128]{1,0:T(8,128)}, f32[40,256]{1,0:T(8,128)}) custom-call(s32[1,4]{1,0:T(1,128)} %lens_ref.1, f32[40,768]{1,0:T(8,128)} %bitcast.15, f32[1,40]{1,0:T(1,128)} %bitcast.17, bf16[768,2560]{1,0:T(8,128)(2,1)} %bitcast.11, bf16[768,2560]{1,0:T(8,128)(2,1)} %bitcast.12, bf16[768,128]{1,0:T(8,128)(2,1)} %bitcast.13, ...), custom_call_target="tpu_custom_call" | custom-call | tf_op jit(solution)/shard_map/pallas_call | solution.py:654
  83.5 4.7 %shard_map.113 = (bf16[768,2560]{1,0:T(8,128)(2,1)}, f32[80,128]{1,0:T(8,128)}, f32[40,256]{1,0:T(8,128)}) custom-call(bf16[768,2560]{1,0:T(8,128)(2,1)} %get-tuple-element.9.x_hbm, f32[80,128]{1,0:T(8,128)} %get-tuple-element.10.p_ref, f32[40,256]{1,0:T(8,128)} %get-tuple-element.11.w_ref), custom_call_target="tpu_custom_call" | custom-call | tf_op jit(solution)/shard_map/pallas_call | solution.py:715

commit v6 on v5

--- a/solution.py
+++ b/solution.py
@@ -18,8 +18,8 @@
 PHEADS = HEADS // PHASES
 PLANES = PHEADS * 64
 PPAIRS = PHEADS // 2
-ROWS = ((0, 16), (16, 40), (16, 40))
-COLS = ((0, 256), (0, 128), (128, 256))
+ROWS = ((16, 40), (16, 40), (0, 16))
+COLS = ((0, 128), (128, 256), (0, 256))
 SLAB = 640
 F32 = jnp.float32
 BF16 = jnp.bfloat16
@@ -438,7 +438,8 @@
             j = t - 1
             chip_copy(j).wait()
             combine(j)
-            each(1, 16, lambda d: out_copy(j, d).start())
+            for d in range(1, 16):
+                out_copy(j, d).start()
             got[j, chip] = comb[j, chip]
 
         @pl.when(t == 2)
@@ -468,7 +469,8 @@
             j = t - 4
             out_all(j).wait()
             scan(j)
-            each(1, 16, lambda d: back_copy(j, d).start())
+            for d in range(1, 16):
+                back_copy(j, d).start()
             ret[j, chip] = back[j, chip]
 
         @pl.when(t == PHASES + 4)
@@ -561,14 +563,14 @@
         part[at, :, :, core] = part[at, :, :, core] + sib[at]
         if s > 0:
             first_x(s).start()
-        for d in (1, 3, 2):
+        for d in (2, 1, 3):
             first_y(s, d).start()
             first_z(s, d).start()
 
     for n in range(2):
         load_li(n).wait()
     bc = bc_v[...]
-    order = (1, 3, 2, 0)
+    order = (2, 1, 3, 0)
     for i, s in enumerate(order):
         at = slab_x(s)
         for n in range(2):
@@ -577,15 +579,14 @@
             out = dot(xg_v[m // 4, :, cols], bc, TN)
             part[at, 2 * n : 2 * n + 2] = out.reshape(2, 4, 2, 40, 256)
             sib_copy(s, n).start()
-        if i == 0:
-            p_chip().wait()
-            pterm[:, :, core] = pterm[:, :, core] + sib_p[...]
-            for d in (1, 3, 2):
-                for q in range(2):
-                    p_first(q, d).start()
-        else:
+        if i > 0:
             settle(order[i - 1])
     settle(0)
+    p_chip().wait()
+    pterm[:, :, core] = pterm[:, :, core] + sib_p[...]
+    for d in (1, 3, 2):
+        for n in range(2):
+            p_first(n, d).start()
 
     def second(n, d):
         if n == 0:
@@ -603,6 +604,18 @@
 
     three = pl.ds(1, 3)
     peers = pl.ds(0, 3)
+    for n in range(3):
+        if n == 0:
+            w_copy(0, 0, 1, r1a, r1a, sibling).wait()
+            s1a[...] = part[group, :, :, core, 16:40, 0:128] + r1a[0] + r1a[1] + r1a[2]
+        elif n == 1:
+            w_copy(1, 0, 1, r1b, r1b, sibling).wait()
+            s1b[...] = part[:, y, :, core, 16:40, 128:256] + r1b[0] + r1b[1] + r1b[2]
+        else:
+            w_copy(2, 0, 1, r1c, r1c, sibling).wait()
+            s1c[...] = part[:, :, z, core, 0:16] + r1c[0] + r1c[1] + r1c[2]
+        for d in (1, 3, 2):
+            second(n, d).start()
     p_copy(0, 0, 1, pterm.at[peers, :, 0, 0:40], pr1a.at[three], sibling).wait()
     p_copy(1, 0, 1, pterm.at[peers, :, 0, 40:80], pr1b.at[three], sibling).wait()
     ps1a[...] = pterm[y, :, core, 0:40] + pr1a[1] + pr1a[2] + pr1a[3]
@@ -611,18 +624,6 @@
         for n in range(2):
             p_second(n, d).start()
 
-    for n in range(3):
-        if n == 0:
-            w_copy(0, 0, 1, r1a, r1a, sibling).wait()
-            s1a[...] = part[group, :, :, core, 0:16] + r1a[0] + r1a[1] + r1a[2]
-        elif n == 1:
-            w_copy(1, 0, 1, r1b, r1b, sibling).wait()
-            s1b[...] = part[:, y, :, core, 16:40, 0:128] + r1b[0] + r1b[1] + r1b[2]
-        else:
-            w_copy(2, 0, 1, r1c, r1c, sibling).wait()
-            s1c[...] = part[:, :, z, core, 16:40, 128:256] + r1c[0] + r1c[1] + r1c[2]
-        for d in (1, 3, 2):
-            second(n, d).start()
     for n, r in enumerate((r2a, r2b, r2c)):
         w_copy(n, 1, 1, r.at[three], r.at[three], sibling).wait()
         if n == 0:
@@ -670,11 +671,11 @@
             f(4, 4, 2, 80, 128), f(4, 4, 80, 128), f(4, 4, 40, 128), f(4, 4, 40, 128),
             f(4, 40, 128), f(4, 40, 128), f(4, 40, 128), f(4, 40, 128),
             f(4, 4, 4, 2, 40, 256), f(4, 4, 4, 40, 256),
-            f(3, 4, 4, 16, 256), f(3, 4, 4, 24, 128), f(3, 4, 4, 24, 128),
-            f(4, 4, 16, 256), f(4, 4, 24, 128), f(4, 4, 24, 128),
-            f(4, 4, 16, 256), f(4, 4, 24, 128), f(4, 4, 24, 128),
-            f(4, 16, 256), f(4, 24, 128), f(4, 24, 128),
-            f(4, 16, 256), f(4, 24, 128), f(4, 24, 128),
+            f(3, 4, 4, 24, 128), f(3, 4, 4, 24, 128), f(3, 4, 4, 16, 256),
+            f(4, 4, 24, 128), f(4, 4, 24, 128), f(4, 4, 16, 256),
+            f(4, 4, 24, 128), f(4, 4, 24, 128), f(4, 4, 16, 256),
+            f(4, 24, 128), f(4, 24, 128), f(4, 16, 256),
+            f(4, 24, 128), f(4, 24, 128), f(4, 16, 256),
             dma(PHASES), dma(PHASES), dma(1), dma(2), dma(2), dma(PHASES), dma(PHASES),
             dma(PHASES), dma(PHASES), dma(2), dma(2), dma(PHASES), dma(PHASES),
             dma(PHASES), dma(PHASES), dma(2), dma(4), dma(4), dma(3, 3), dma(3, 3), dma(3, 2), dma(3, 2),

time: 88.9 us -> 88.4 us (level)
  no operation moved by 1% of the time
where the time goes in v6:
time: 88.4 us; the launch traced here: 88.2 us
  Pallas kernels  87.6 us (99%)
    pallas_call x1, Pallas kernels, layer(): pl.pallas_call(layer_kernel, in_specs=[pl.BlockSpec(memory_space=pltpu.SM...  82.9 us
    pallas_call x1, Pallas kernels, deliver(): pl.pallas_call(deliver_kernel, in_specs=[a, v, v], out_specs=[a, v, v], o...  4.74 us

profile of v6, /device:TPU:0, one launch (start us, length us, event | category | flops | bytes accessed | tf_op | source)
XLA Modules:
  0.0 88.2 jit_solution(2943101535841330023)
XLA Ops:
  0.6 82.9 %shard_map.112 = (bf16[768,2560]{1,0:T(8,128)(2,1)}, f32[80,128]{1,0:T(8,128)}, f32[40,256]{1,0:T(8,128)}) custom-call(s32[1,4]{1,0:T(1,128)} %lens_ref.1, f32[40,768]{1,0:T(8,128)} %bitcast.15, f32[1,40]{1,0:T(1,128)} %bitcast.17, bf16[768,2560]{1,0:T(8,128)(2,1)} %bitcast.11, bf16[768,2560]{1,0:T(8,128)(2,1)} %bitcast.12, bf16[768,128]{1,0:T(8,128)(2,1)} %bitcast.13, ...), custom_call_target="tpu_custom_call" | custom-call | tf_op jit(solution)/shard_map/pallas_call | solution.py:655
  83.5 4.7 %shard_map.113 = (bf16[768,2560]{1,0:T(8,128)(2,1)}, f32[80,128]{1,0:T(8,128)}, f32[40,256]{1,0:T(8,128)}) custom-call(bf16[768,2560]{1,0:T(8,128)(2,1)} %get-tuple-element.9.x_hbm, f32[80,128]{1,0:T(8,128)} %get-tuple-element.10.p_ref, f32[40,256]{1,0:T(8,128)} %get-tuple-element.11.w_ref), custom_call_target="tpu_custom_call" | custom-call | tf_op jit(solution)/shard_map/pallas_call | solution.py:716
